TPU v7x, 512 devices: a whole 4x8x8 slice. The times are simulated.
512 devices in a mesh: remap: 2 (over core), grid: 256 (over z, y, x).
Axes of the slice: x: 4, y: 8, z: 8, core: 2. Of those that a mesh axis runs over, the one named last changes fastest.
Arguments:
- tensor: bfloat16 [256, 256, 128, 128], P('grid', None, 'remap'), may hold values from -0.5 to 0.5
- go_blocks: bfloat16 [256, 2, 128, 128], P('grid'), may hold values from -0.5 to 0.5
- gv_blocks: bfloat16 [256, 2, 128, 128], P('grid'), may hold values from -0.5 to 0.5
- partners: int32 [256, 2], P('grid'), may hold values from 0 to 255, as said below
Outputs:
- chi: float32 [256, 2, 256, 256], P('grid', None, 'remap')
Inputs may be any that keep to these rules, and one draw needn't show every extreme that they name: `partners`: the 2 entries of a row are distinct blocks; block b belongs to grid index b, and each partner's grid index is at most 1 away from its block's, counted cyclically.
All inputs are finite; a program needn't handle non-finite values.
Results may differ from a plain program's by a relative error of at most 0.004.
Values may be sent and summed in bfloat16 or wider, within the bound.
A program may use at most 128 MiB of HBM per device.

v0:
```python
import jax
import jax.numpy as jnp
from jax import lax
from jax.sharding import PartitionSpec as P

REACH = 1


def passed_along(shard, axis, by):
    length = lax.axis_size(axis)
    return lax.ppermute(shard, axis, [(i, (i + by) % length) for i in range(length)])


def on_device(tensor, go_blocks, gv_blocks, partners):
    blocks_here, ri_count, rows_here, block_size = tensor.shape
    slot_count = partners.shape[1]
    grid_count = lax.axis_size("grid")
    position = lax.axis_index("grid")
    pieces = []
    for offset in range(-REACH, REACH + 1):
        if offset == 0:
            pieces.append(tensor)
        else:
            pieces.append(passed_along(tensor, "grid", -offset))
    owners = partners // blocks_here
    distance = ((owners - position + REACH) % grid_count).reshape(-1)
    chosen_list = []
    for slot_index in range(blocks_here * slot_count):
        picked = jnp.zeros_like(tensor[0])
        for place in range(len(pieces)):
            candidate = pieces[place][0]
            picked = jnp.where(distance[slot_index] == place, candidate, picked)
        chosen_list.append(picked)
    partner_tensor = jnp.stack(chosen_list, axis=0)
    green_virt = gv_blocks.reshape(blocks_here * slot_count, block_size, block_size)
    virtual = jnp.einsum(
        "sqnm,sml->sqnl", partner_tensor, green_virt, preferred_element_type=jnp.float32
    ).astype(jnp.bfloat16)
    occupied = jnp.einsum(
        "aplm,acmn->acpln", tensor, go_blocks, preferred_element_type=jnp.float32
    ).astype(jnp.bfloat16)
    occ_side = occupied.reshape(blocks_here * slot_count, ri_count, rows_here, block_size)
    virt_side = lax.all_to_all(virtual, "remap", split_axis=3, concat_axis=2, tiled=True)
    share = ri_count // lax.axis_size("remap")
    summed = lax.psum_scatter(
        jnp.einsum("spln,sqnl->psq", occ_side, virt_side, preferred_element_type=jnp.float32),
        "remap",
        scatter_dimension=0,
        tiled=True,
    )
    return jnp.transpose(summed, (1, 0, 2)).reshape(blocks_here, slot_count, share, ri_count)


def solution(mesh):
    placed = (
        P("grid", None, "remap", None),
        P("grid", None, None, None),
        P("grid", None, None, None),
        P("grid", None),
    )
    return jax.shard_map(
        on_device,
        mesh=mesh,
        in_specs=placed,
        out_specs=P("grid", None, "remap", None),
        check_vma=False,
    )
```

profile of v0, /device:TPU:1, one launch (start us, length us, event | category | flops | bytes accessed | tf_op | source)
XLA Modules:
  0.0 221.1 jit_solution(17442215048470822023)
XLA Ops:
  6.5 0.0 copy-start
  6.5 0.0 copy-start.4
  6.5 0.0 reduce-scatter.2.cloned.1.call-start
  6.5 6.9 %copy.25 = bf16[1,256,64,128]{3,1,2,0:T(8,128)(2,1)} copy(bf16[1,256,64,128]{3,2,1,0:T(8,128)(2,1)} %param.4) | data formatting | bytes 8388608 | tf_op args[0]
  13.4 3.9 %collective-permute-start.1 = (bf16[1,256,64,128]{3,1,2,0:T(8,128)(2,1)}, bf16[1,256,64,128]{3,1,2,0:T(8,128)(2,1)}, u32[]{:S(2)}, u32[]{:S(2)}) collective-permute-start(bf16[1,256,64,128]{3,1,2,0:T(8,128)(2,1)} %copy.25), channel_id=1, source_target_pairs={{0,1},{1,2},{2,3},{3,4},{4,5},{5,6},{6,7},{7,8},{8,9},{9,10},{10,1... | collective-permute-start | bytes 12582920 | tf_op jit(solution)/shard_map/ppermute | solution.py:11
  17.4 14.6 %collective-permute-start = (bf16[1,256,64,128]{3,1,2,0:T(8,128)(2,1)}, bf16[1,256,64,128]{3,1,2,0:T(8,128)(2,1)}, u32[]{:S(2)}, u32[]{:S(2)}) collective-permute-start(bf16[1,256,64,128]{3,1,2,0:T(8,128)(2,1)} %copy.25), channel_id=1, source_target_pairs={{0,255},{1,0},{2,1},{3,2},{4,3},{5,4},{6,5},{7,6},{8,7},{9,8},{10,... | collective-permute-start | bytes 12582920 | tf_op jit(solution)/shard_map/ppermute | solution.py:11
  31.9 0.0 copy-done.4
  32.0 0.6 fusion.18
  36.4 0.0 copy-done
  36.4 0.0 copy-start.2
  36.5 10.8 %convert_bitcast_fusion = bf16[2,256,64,128]{1,3,2,0:T(8,128)(2,1)} fusion(bf16[256,64,128]{2,1,0:T(8,128)(2,1)} %bitcast.42, bf16[1,2,128,128]{3,2,1,0:T(8,128)(2,1)S(1)} %copy-done), kind=kOutput, calls=%fused_computation.6 | convolution fusion | flops 1077936128 | bytes 12648448 | tf_op jit(solution)/shard_map/aplm,acmn->acpln/dot_general | solution.py:39
  47.3 73.3 %collective-permute-done.1 = bf16[1,256,64,128]{3,1,2,0:T(8,128)(2,1)} collective-permute-done((bf16[1,256,64,128]{3,1,2,0:T(8,128)(2,1)}, bf16[1,256,64,128]{3,1,2,0:T(8,128)(2,1)}, u32[]{:S(2)}, u32[]{:S(2)}) %collective-permute-start.1) | collective-permute-done | bytes 4194336 | tf_op jit(solution)/shard_map/ppermute | solution.py:11
  120.6 0.9 collective-permute-done
  121.5 0.0 copy-done.2
  121.5 0.0 copy-start.3
  121.5 12.9 %select_select_fusion.1 = (bf16[1,256,64,128]{3,1,2,0:T(8,128)(2,1)S(1)}, bf16[1,256,64,128]{3,1,2,0:T(8,128)(2,1)}) fusion(bf16[1,256,64,128]{3,1,2,0:T(8,128)(2,1)} %collective-permute-done, bf16[1,256,64,128]{3,1,2,0:T(8,128)(2,1)} %collective-permute-done.1, pred[]{:T(512)} %bitcast.2, pred[]{:T(512)} %bitcast.1, pred[]{:T(512)} %bitcast, ...), kind=kLoop, calls=%fused_computation.11 | loop fusion | flops 12582912 | bytes 20971526 | tf_op jit(solution)/shard_map/jit(_where)/select_n | solution.py:32
  134.4 0.0 copy-done.3
  134.4 7.8 %fusion.6 = bf16[2,256,64,128]{3,1,2,0:T(8,128)(2,1)} fusion(bf16[1,256,64,128]{3,1,2,0:T(8,128)(2,1)} %get-tuple-element.6, bf16[1,256,64,128]{3,1,2,0:T(8,128)(2,1)S(1)} %get-tuple-element.5, bf16[1,2,128,128]{3,2,1,0:T(8,128)(2,1)S(1)} %copy-done.3), kind=kOutput, calls=%fused_computation.7 | convolution fusion | flops 1082130432 | bytes 16842752 | tf_op jit(solution)/shard_map/sqnm,sml->sqnl/dot_general | solution.py:36
  142.1 12.3 %copy.29 = bf16[2,256,64,128]{1,2,0,3:T(8,128)(2,1)} copy(bf16[2,256,64,128]{3,1,2,0:T(8,128)(2,1)} %fusion.6) | data formatting | bytes 16777216 | tf_op jit(solution)/shard_map/convert_element_type | solution.py:38
  154.4 19.7 %all_to_all.18 = bf16[2,256,64,128]{1,2,0,3:T(8,128)(2,1)} all-to-all(bf16[2,256,64,128]{1,2,0,3:T(8,128)(2,1)} %copy.29), channel_id=1, replica_groups=mesh['remap'=2,'grid'=256] {'remap'}, dimensions={3} | all-to-all | bytes 16777216 | tf_op jit(solution)/shard_map/all_to_all | solution.py:43
  174.0 11.5 %copy.31 = bf16[2,256,2,64,64]{1,4,3,2,0:T(8,128)(2,1)} copy(bf16[2,256,2,64,64]{1,3,0,4,2:T(8,128)(2,1)} %bitcast.43) | data formatting | bytes 16777216 | tf_op jit(solution)/shard_map/all_to_all | solution.py:43
  185.5 0.0 copy-start.1
  185.5 13.3 %fusion.11 = f32[256,2,256]{0,2,1:T(8,128)} fusion(bf16[2,256,128,64]{1,3,2,0:T(8,128)(2,1)} %bitcast.44, bf16[2,256,64,128]{1,3,2,0:T(8,128)(2,1)} %convert_bitcast_fusion), kind=kOutput, calls=%fused_computation.12 | convolution fusion | flops 2147483648 | bytes 17301504 | tf_op jit(solution)/shard_map/spln,sqnl->psq/dot_general | solution.py:46
  198.8 0.0 reduce-scatter.2.cloned.1.call-update
  198.8 13.6 %reduce-scatter.2.cloned.1.call-done = f32[128,2,256]{0,2,1:T(8,128)} async-done(((f32[256,2,256]{0,2,1:T(8,128)}), f32[128,2,256]{0,2,1:T(8,128)}) %reduce-scatter.2.cloned.1.call-update) | async-done | bytes 262160 | tf_op jit(solution)/shard_map/reduce_scatter | solution.py:45
  212.5 1.8 copy.35
  214.3 0.0 copy-done.1
  (1 shorter events, 0.0 us)
Async XLA Ops:
  6.5 29.9 %copy-start = (bf16[1,2,128,128]{3,2,1,0:T(8,128)(2,1)S(1)}, bf16[1,2,128,128]{3,2,1,0:T(8,128)(2,1)}, u32[]{:S(2)}) copy-start(bf16[1,2,128,128]{3,2,1,0:T(8,128)(2,1)} %param.5) | copy-start | bytes 196612
  6.5 25.4 %copy-start.4 = (s32[1,2]{1,0:T(1,128)S(1)}, s32[1,2]{1,0:T(1,128)}, u32[]{:S(2)}) copy-start(s32[1,2]{1,0:T(1,128)} %param.7) | copy-start | bytes 28
  6.5 205.9 %reduce-scatter.2.cloned.1.call-start = ((), (), s32[]{:S(2)}) async-start(), calls=%async_computation.2 | async-start | bytes 786432 | tf_op jit(solution)/shard_map/reduce_scatter | solution.py:45
  13.4 107.2 %collective-permute-start.1 = (bf16[1,256,64,128]{3,1,2,0:T(8,128)(2,1)}, bf16[1,256,64,128]{3,1,2,0:T(8,128)(2,1)}, u32[]{:S(2)}, u32[]{:S(2)}) collective-permute-start(bf16[1,256,64,128]{3,1,2,0:T(8,128)(2,1)} %copy.25), channel_id=1, source_target_pairs={{0,1},{1,2},{2,3},{3,4},{4,5},{5,6},{6,7},{7,8},{8,9},{9,10},{10,1... | collective-permute-start | bytes 12582920 | tf_op jit(solution)/shard_map/ppermute | solution.py:11
  17.4 104.1 %collective-permute-start = (bf16[1,256,64,128]{3,1,2,0:T(8,128)(2,1)}, bf16[1,256,64,128]{3,1,2,0:T(8,128)(2,1)}, u32[]{:S(2)}, u32[]{:S(2)}) collective-permute-start(bf16[1,256,64,128]{3,1,2,0:T(8,128)(2,1)} %copy.25), channel_id=1, source_target_pairs={{0,255},{1,0},{2,1},{3,2},{4,3},{5,4},{6,5},{7,6},{8,7},{9,8},{10,... | collective-permute-start | bytes 12582920 | tf_op jit(solution)/shard_map/ppermute | solution.py:11
  36.4 85.0 %copy-start.2 = (bf16[1,256,64,128]{3,2,1,0:T(8,128)(2,1)S(1)}, bf16[1,256,64,128]{3,2,1,0:T(8,128)(2,1)}, u32[]{:S(2)}) copy-start(bf16[1,256,64,128]{3,2,1,0:T(8,128)(2,1)} %param.4) | copy-start | bytes 12582916
  121.5 12.9 %copy-start.3 = (bf16[1,2,128,128]{3,2,1,0:T(8,128)(2,1)S(1)}, bf16[1,2,128,128]{3,2,1,0:T(8,128)(2,1)}, u32[]{:S(2)}) copy-start(bf16[1,2,128,128]{3,2,1,0:T(8,128)(2,1)} %param.6) | copy-start | bytes 196612
  185.5 28.7 %copy-start.1 = (bf16[1,2,128,128]{3,2,1,0:T(8,128)(2,1)S(1)}, bf16[1,2,128,128]{3,2,1,0:T(8,128)(2,1)}, u32[]{:S(2)}) copy-start(bf16[1,2,128,128]{3,2,1,0:T(8,128)(2,1)} %param.5) | copy-start | bytes 196612
Sparse Core Ops, SparseCore 0:
  199.0 13.4 reduce-scatter.1
where the time goes:
time: 222 us; the launch traced here: 221 us
  waiting for transfers between devices  87.9 us (40%)
  local copies, waits for them, and re-layouts  33.1 us (15%)
  matrix products  31.8 us (14%)
  blocking collectives  19.7 us (9%)
  starting transfers between devices  18.5 us (8%)
  between operations  17.3 us (8%)
  other arithmetic  12.9 us (6%)
    ppermute x2, waiting for transfers between devices, passed_along(): lax.ppermute(shard, axis, [(i, (i + by) % length) for i in range(length)])  74.2 us
    all_to_all x1, blocking collectives, on_device(): lax.all_to_all(virtual, 'remap', split_axis=3, concat_axis=2, tiled=True)  19.7 us
    ppermute x2, starting transfers between devices, passed_along(): lax.ppermute(shard, axis, [(i, (i + by) % length) for i in range(length)])  18.5 us
    reduce_scatter x1, waiting for transfers between devices, on_device(): lax.psum_scatter(jnp.einsum('spln,sqnl->psq', occ_side, virt_side, prefer...  13.6 us
    dot_general x1, matrix products, on_device(): jnp.einsum('spln,sqnl->psq', occ_side, virt_side, preferred_element_type=...  13.3 us
    select_n x1, other arithmetic, on_device(): picked = jnp.where(distance[slot_index] == place, candidate, picked)  12.9 us
    convert_element_type x1, local copies, waits for them, and re-layouts, on_device(): virtual = jnp.einsum('sqnm,sml->sqnl', partner_tensor, green_virt, prefer...  12.3 us
    all_to_all x1, local copies, waits for them, and re-layouts, on_device(): lax.all_to_all(virtual, 'remap', split_axis=3, concat_axis=2, tiled=True)  11.5 us
  transfers between devices with their start and end apart: 3, of which 3 were waited for; matrix products, arithmetic and copies ran while one was open for 5% of the time, Pallas kernels for 0%

commit v1 on v0

v1 whole, which is shorter than its diff:
```python
import jax
import jax.numpy as jnp
from jax import lax
from jax.experimental import pallas as pl
from jax.experimental.pallas import tpu as pltpu
from jax.sharding import PartitionSpec as P

MESH = pl.DeviceIdType.MESH
BF = jnp.bfloat16
F32 = jnp.float32
BS = 128

KEEP1 = 18
KEEP2 = 20
RAW_BOUNDS = (0, 8, 16, 24, 32, 40, 44, 46)
FIRST_BOUNDS = (46, 54, 64)
SECOND_BOUNDS = (44, 54, 64)
SIBLING_CHUNKS = 4

RIGHT, LEFT, SELF = 0, 1, 2


def nt(a, b):
    return lax.dot_general(a, b, (((1,), (1,)), ((), ())), preferred_element_type=F32)


def kernel(
    tensor, go_ref, gv_ref, partners, out,
    traw, rows, far, occ, trans, got2, perm, green, gsend, gfar, first, second,
    acc_right, acc_left, acc_self, part_right, part_left, ret_right, ret_left,
    fin_send, fin_recv, load_sem, send_sem, recv_sem,
):
    half = rows.shape[0]
    ri = rows.shape[1]
    share = ri // 2
    count = lax.axis_size("grid")
    grid_at = lax.axis_index("grid")
    core = lax.axis_index("remap")
    right = lax.rem(grid_at + 1, count)
    left = lax.rem(grid_at + count - 1, count)
    other = 1 - core

    load = pltpu.make_async_copy(tensor.at[0], traw.at[core], load_sem)
    load.start()

    barrier = pltpu.get_barrier_semaphore()
    for target in ({"grid": left}, {"grid": right}, {"remap": other}):
        pl.semaphore_signal(barrier, inc=1, device_id=target, device_id_type=MESH)

    used = [0]

    def remote(source, target, device):
        at = used[0]
        used[0] += 1
        return pltpu.make_async_remote_copy(
            src_ref=source, dst_ref=target, send_sem=send_sem.at[at], recv_sem=recv_sem.at[at],
            device_id=device, device_id_type=MESH,
        )

    to_left, to_right, to_other = {"grid": left}, {"grid": right}, {"remap": other}
    greens = remote(gsend, gfar, to_left)
    step = ri // SIBLING_CHUNKS
    siblings = [
        remote(tensor.at[0, pl.ds(i * step, step)], traw.at[core, pl.ds(i * step, step)], to_other)
        for i in range(SIBLING_CHUNKS)
    ]
    raws = [
        remote(rows.at[pl.ds(a, b - a)], far.at[pl.ds(a, b - a)], to_left)
        for a, b in zip(RAW_BOUNDS[:-1], RAW_BOUNDS[1:])
    ]
    firsts = [
        remote(trans.at[0, pl.ds(a, b - a)], first.at[pl.ds(a - FIRST_BOUNDS[0], b - a)], to_right)
        for a, b in zip(FIRST_BOUNDS[:-1], FIRST_BOUNDS[1:])
    ]
    seconds = [
        remote(trans.at[1, pl.ds(a, b - a)], second.at[pl.ds(a - SECOND_BOUNDS[0], b - a)], to_right)
        for a, b in zip(SECOND_BOUNDS[:-1], SECOND_BOUNDS[1:])
    ]
    back_right = remote(part_right, ret_right, to_left)
    back_left = remote(part_left, ret_left, to_right)
    finals = [remote(fin_send.at[d], fin_recv.at[d], to_other) for d in (RIGHT, LEFT, SELF)]

    def picked(ref, target):
        total = jnp.zeros((BS, BS), F32)
        for slot in range(2):
            weight = (partners[0, slot] == target).astype(F32)
            total = total + ref[0, slot].astype(F32) * weight
        return total.astype(BF)

    gsend[0] = picked(go_ref, left)
    gsend[1] = picked(gv_ref, left)

    out_row = lax.broadcasted_iota(jnp.int32, (256, 256), 0)
    in_row = lax.broadcasted_iota(jnp.int32, (256, 256), 1)
    perm[...] = (in_row == (out_row & 15) * 16 + (out_row >> 4)).astype(F32).astype(BF)

    pl.semaphore_wait(barrier, 3)
    greens.start()
    for copy in siblings:
        copy.start()

    n_at = lax.broadcasted_iota(jnp.int32, (half, BS), 0) + core * half
    n_of = lax.broadcasted_iota(jnp.int32, (half, BS), 1)
    choose = (n_at == n_of).astype(F32).astype(BF)
    green[pl.ds(0, half)] = nt(choose, picked(go_ref, right)).astype(BF)
    green[pl.ds(2 * half, half)] = nt(choose, picked(go_ref, grid_at)).astype(BF)
    empty = jnp.zeros((BS, BS), BF)

    def doubled(block):
        top = jnp.concatenate([block, empty], axis=1)
        bottom = jnp.concatenate([empty, block], axis=1)
        return jnp.concatenate([top, bottom], axis=0)

    got2[0] = doubled(picked(gv_ref, right))
    got2[2] = doubled(picked(gv_ref, grid_at))

    load.wait()

    def turn(n0):
        def body(i, carry):
            q0 = pl.multiple_of(i * 32, 32)
            pair = [
                traw[core, pl.ds(q0 + 16 * j, 16), pl.ds(n0, 16), :].reshape(256, BS) for j in range(2)
            ]
            turned = jnp.dot(perm[...], jnp.concatenate(pair, axis=1), preferred_element_type=F32).astype(BF)
            for j in range(2):
                rows[pl.ds(n0, 16), pl.ds(q0 + 16 * j, 16), :] = turned[:, j * BS:(j + 1) * BS].reshape(16, 16, BS)
            return carry

        lax.fori_loop(0, ri // 32, body, 0)

    sent = 0
    for n0 in range(0, half, 16):
        turn(n0)
        while sent < len(raws) and RAW_BOUNDS[sent + 1] <= n0 + 16:
            raws[sent].start()
            sent += 1

    greens.wait_recv()
    green[pl.ds(half, half)] = nt(choose, gfar[1]).astype(BF)
    got2[1] = doubled(gfar[0])

    def first_product(i, carry):
        p0 = pl.multiple_of(i * 8, 8)
        tiles = []
        for j in range(8):
            tiles.append(traw[0, p0 + j])
            tiles.append(traw[1, p0 + j])
        product = nt(green[...], jnp.concatenate(tiles, axis=0)).astype(BF)
        for j in range(8):
            occ[p0 + j] = product[:, j * BS:(j + 1) * BS]
        return carry

    for i in range(SIBLING_CHUNKS):
        siblings[i].wait_recv()
        lax.fori_loop(i * step // 8, (i + 1) * step // 8, first_product, 0)

    def second_product(direction, n0):
        def body(i, carry):
            for u in range(2):
                p0 = pl.multiple_of(i * 32 + u * 16, 16)
                pair = [
                    occ[pl.ds(p0, 16), pl.ds(direction * half + n0 + 16 * j, 16), :].reshape(256, BS)
                    for j in range(2)
                ]
                turned = jnp.dot(perm[...], jnp.concatenate(pair, axis=1), preferred_element_type=F32).astype(BF)
                product = nt(turned, got2[direction]).astype(BF)
                for j in range(2):
                    trans[direction, pl.ds(n0 + 16 * j, 16), pl.ds(p0, 16), :] = (
                        product[:, j * BS:(j + 1) * BS].reshape(16, 16, BS)
                    )
            return carry

        lax.fori_loop(0, ri // 32, body, 0)

    second_product(0, 32)
    for copy in firsts:
        copy.start()
    second_product(1, 32)
    for copy in seconds:
        copy.start()

    def wide(ref, at, many):
        return jnp.concatenate([ref[at + j] for j in range(many)], axis=1)

    def contract(acc, x, x0, y, y0, size, clear=False):
        if clear:
            acc[...] = jnp.zeros_like(acc)
        groups, rest = divmod(size, 4)

        def body(i, carry):
            acc[...] += nt(wide(x, x0 + 4 * i, 4), wide(y, y0 + 4 * i, 4))
            return carry

        if groups:
            lax.fori_loop(0, groups, body, 0)
        if rest:
            acc[...] += nt(wide(x, x0 + 4 * groups, rest), wide(y, y0 + 4 * groups, rest))

    second_product(0, 0)
    second_product(1, 0)

    def raw_chunk(i):
        a, b = RAW_BOUNDS[i], RAW_BOUNDS[i + 1]
        raws[i].wait_recv()
        contract(acc_right, trans.at[0], a, far, a, b - a, clear=i == 0)
        if b <= SECOND_BOUNDS[0]:
            contract(part_left, far, a, trans.at[1], a, b - a, clear=i == 0)

    raw_chunk(0)
    second_product(2, 32)
    second_product(2, 0)
    raw_chunk(1)
    contract(acc_self, trans.at[2], 0, rows, 0, half, clear=True)
    fin_send[SELF] = acc_self[pl.ds(pl.multiple_of(other * share, share), share), :]
    finals[SELF].start()

    raw_chunk(2)
    raw_chunk(3)
    for i, copy in enumerate(firsts):
        a, b = FIRST_BOUNDS[i], FIRST_BOUNDS[i + 1]
        copy.wait_recv()
        contract(part_right, first, a - FIRST_BOUNDS[0], rows, a, b - a, clear=i == 0)
    back_right.start()
    raw_chunk(4)
    raw_chunk(5)
    back_left.start()
    raw_chunk(6)
    for i, copy in enumerate(seconds):
        a, b = SECOND_BOUNDS[i], SECOND_BOUNDS[i + 1]
        copy.wait_recv()
        contract(acc_left, rows, a, second, a - SECOND_BOUNDS[0], b - a, clear=i == 0)

    theirs = pl.ds(pl.multiple_of(other * share, share), share)
    mine = pl.ds(pl.multiple_of(core * share, share), share)
    back_right.wait_recv()
    fin_send[RIGHT] = acc_right[theirs, :] + ret_right[theirs, :]
    finals[RIGHT].start()
    back_left.wait_recv()
    fin_send[LEFT] = acc_left[theirs, :] + ret_left[theirs, :]
    finals[LEFT].start()
    finals[SELF].wait_recv()
    out[SELF] = acc_self[mine, :] + fin_recv[SELF]
    finals[RIGHT].wait_recv()
    out[RIGHT] = acc_right[mine, :] + ret_right[mine, :] + fin_recv[RIGHT]
    finals[LEFT].wait_recv()
    out[LEFT] = acc_left[mine, :] + ret_left[mine, :] + fin_recv[LEFT]

    for copy in [greens, *siblings, *raws, *firsts, *seconds, back_right, back_left, *finals]:
        copy.wait_send()


COPIES = 1 + SIBLING_CHUNKS + len(RAW_BOUNDS) + len(FIRST_BOUNDS) + len(SECOND_BOUNDS) - 3 + 2 + 3


def on_device(tensor, go_blocks, gv_blocks, partners):
    _, ri, half, _ = tensor.shape
    share = ri // 2
    square = pltpu.VMEM((ri, ri), F32)
    vmem = pl.BlockSpec(memory_space=pltpu.VMEM)
    parts = pl.pallas_call(
        kernel,
        out_shape=jax.ShapeDtypeStruct((3, share, ri), F32),
        in_specs=[pl.BlockSpec(memory_space=pl.ANY), vmem, vmem, pl.BlockSpec(memory_space=pltpu.SMEM)],
        out_specs=vmem,
        scratch_shapes=[
            pltpu.VMEM((2, ri, half, BS), BF),
            pltpu.VMEM((half, ri, BS), BF),
            pltpu.VMEM((half - KEEP1, ri, BS), BF),
            pltpu.VMEM((ri, 3 * half, BS), BF),
            pltpu.VMEM((3, half, ri, BS), BF),
            pltpu.VMEM((3, 2 * BS, 2 * BS), BF),
            pltpu.VMEM((256, 256), BF),
            pltpu.VMEM((3 * half, BS), BF),
            pltpu.VMEM((2, BS, BS), BF),
            pltpu.VMEM((2, BS, BS), BF),
            pltpu.VMEM((KEEP1, ri, BS), BF),
            pltpu.VMEM((KEEP2, ri, BS), BF),
            square, square, square, square, square, square, square,
            pltpu.VMEM((3, share, ri), F32),
            pltpu.VMEM((3, share, ri), F32),
            pltpu.SemaphoreType.DMA,
            pltpu.SemaphoreType.DMA((COPIES,)),
            pltpu.SemaphoreType.DMA((COPIES,)),
        ],
        compiler_params=pltpu.CompilerParams(
            collective_id=0, has_side_effects=True, vmem_limit_bytes=58 * 1024 * 1024
        ),
    )(tensor, go_blocks, gv_blocks, partners)
    count = lax.axis_size("grid")
    grid_at = lax.axis_index("grid")
    where_to = partners[0][:, None, None]
    chosen = jnp.where(
        where_to == lax.rem(grid_at + 1, count),
        parts[RIGHT][None],
        jnp.where(where_to == grid_at, parts[SELF][None], parts[LEFT][None]),
    )
    return chosen[None]


def solution(mesh):
    placed = (
        P("grid", None, "remap", None),
        P("grid", None, None, None),
        P("grid", None, None, None),
        P("grid", None),
    )
    return jax.shard_map(
        on_device,
        mesh=mesh,
        in_specs=placed,
        out_specs=P("grid", None, "remap", None),
        check_vma=False,
    )
```

time: 222 us -> 102 us (0.46)
  Pallas kernels: 0 us -> 99.6 us
  waiting for transfers between devices: 87.9 us -> 0 us
  local copies, waits for them, and re-layouts: 33.1 us -> 1.06 us
  matrix products: 31.8 us -> 0 us
  blocking collectives: 19.7 us -> 0 us
  starting transfers between devices: 18.5 us -> 0 us
  between operations: 17.3 us -> 0.03 us
  other arithmetic: 12.9 us -> 0.8 us
    pallas_call x0 -> x1, Pallas kernels: none -> 99.6 us  [on_device(): pl.pallas_call(kernel, out_shape=jax.ShapeDtypeStruct((3, share, ri), F32...]
    ppermute x2 -> x0, waiting for transfers between devices: 74.2 us -> none  [passed_along(): lax.ppermute(shard, axis, [(i, (i + by) % length) for i in range(length)])]
    dot_general x3 -> x0, matrix products: 31.8 us -> none  [the longest x1 13.3 us: on_device(): jnp.einsum('spln,sqnl->psq', occ_side, virt_side, preferred_element_type=...]
    all_to_all x1 -> x0, blocking collectives: 19.7 us -> none  [on_device(): lax.all_to_all(virtual, 'remap', split_axis=3, concat_axis=2, tiled=True)]
    ppermute x2 -> x0, starting transfers between devices: 18.5 us -> none  [passed_along(): lax.ppermute(shard, axis, [(i, (i + by) % length) for i in range(length)])]
    reduce_scatter x1 -> x0, waiting for transfers between devices: 13.6 us -> none  [on_device(): lax.psum_scatter(jnp.einsum('spln,sqnl->psq', occ_side, virt_side, prefer...]
    convert_element_type x1 -> x0, local copies, waits for them, and re-layouts: 12.3 us -> none  [on_device(): virtual = jnp.einsum('sqnm,sml->sqnl', partner_tensor, green_virt, prefer...]
    select_n x2 -> x1, other arithmetic: 12.9 us -> 0.8 us  [on_device(): jnp.where(where_to == lax.rem(grid_at + 1, count), parts[RIGHT][None], jn...]
  transfers between devices with their start and end apart: 3 -> 0, of which waited for: 3 -> 0; matrix products, arithmetic and copies ran while one was open for 5% -> 0% of each run, Pallas kernels for 0% -> 0%
where the time goes in v1:
time: 102 us; the launch traced here: 101 us
  Pallas kernels  99.6 us (98%)
  local copies, waits for them, and re-layouts  1.06 us (1%)
    pallas_call x1, Pallas kernels, on_device(): pl.pallas_call(kernel, out_shape=jax.ShapeDtypeStruct((3, share, ri), F32...  99.6 us

profile of v1, /device:TPU:1, one launch (start us, length us, event | category | flops | bytes accessed | tf_op | source)
XLA Modules:
  0.0 101.5 jit_solution(16070730081213580187)
XLA Ops:
  0.0 0.0 copy-start
  0.0 99.6 %shard_map.46 = f32[3,128,256]{2,1,0:T(8,128)} custom-call(bf16[1,256,64,128]{3,2,1,0:T(8,128)(2,1)} %tensor.1, bf16[1,2,128,128]{3,2,1,0:T(8,128)(2,1)} %go_ref.1, bf16[1,2,128,128]{3,2,1,0:T(8,128)(2,1)} %gv_ref.1, s32[1,2]{1,0:T(1,128)} %partners.1), custom_call_target="tpu_custom_call" | custom-call | tf_op jit(solution)/shard_map/pallas_call | solution.py:261
  99.6 1.1 %slice_bitcast_fusion.2 = (f32[128,256]{1,0:T(8,128)S(1)}, f32[128,256]{1,0:T(8,128)S(1)}, f32[128,256]{1,0:T(8,128)S(1)}) fusion(f32[3,128,256]{2,1,0:T(8,128)} %shard_map.46), kind=kLoop, calls=%fused_computation.3 | loop fusion | bytes 786432 | tf_op jit(solution)/shard_map/jit(_where)/broadcast_in_dim | solution.py:293
  100.6 0.0 copy-done
  100.7 0.8 select_select_fusion
  (1 shorter events, 0.0 us)
Async XLA Ops:
  0.0 100.6 %copy-start = (s32[1,2]{1,0:T(1,128)S(1)}, s32[1,2]{1,0:T(1,128)}, u32[]{:S(2)}) copy-start(s32[1,2]{1,0:T(1,128)} %partners.1) | copy-start | bytes 28

commit v2 on v1

--- a/solution.py
+++ b/solution.py
@@ -10,12 +10,12 @@
 F32 = jnp.float32
 BS = 128
 
-KEEP1 = 18
-KEEP2 = 20
-RAW_BOUNDS = (0, 8, 16, 24, 32, 40, 44, 46)
-FIRST_BOUNDS = (46, 54, 64)
-SECOND_BOUNDS = (44, 54, 64)
-SIBLING_CHUNKS = 4
+KEEP1 = 20
+KEEP2 = 22
+RAW_BOUNDS = (0, 8, 16, 24, 32, 38, 42, 44)
+FIRST_FROM = 64 - KEEP1
+SECOND_BOUNDS = (42, 54, 64)
+P_CHUNKS = 4
 
 RIGHT, LEFT, SELF = 0, 1, 2
 
@@ -25,9 +25,10 @@
 
 
 def kernel(
-    tensor, go_ref, gv_ref, partners, out,
+    tensor, go_ref, gv_ref, partners, out_right, out_left, out_self,
     traw, rows, far, occ, trans, got2, perm, green, gsend, gfar, first, second,
-    acc_right, acc_left, acc_self, part_right, part_left, ret_right, ret_left,
+    acc_right, acc_left, acc_self, part_right, part_left,
+    back_right_send, back_left_send, ret_right, ret_left,
     fin_send, fin_recv, load_sem, send_sem, recv_sem,
 ):
     half = rows.shape[0]
@@ -40,8 +41,13 @@
     left = lax.rem(grid_at + count - 1, count)
     other = 1 - core
 
-    load = pltpu.make_async_copy(tensor.at[0], traw.at[core], load_sem)
-    load.start()
+    def loaded(at, n0, size):
+        span = pl.ds(n0, size)
+        return pltpu.make_async_copy(tensor.at[0, :, span], traw.at[core, :, span], load_sem.at[at])
+
+    loads = [loaded(0, 0, 16), loaded(1, 16, half - 16)]
+    for copy in loads:
+        copy.start()
 
     barrier = pltpu.get_barrier_semaphore()
     for target in ({"grid": left}, {"grid": right}, {"remap": other}):
@@ -59,25 +65,29 @@
 
     to_left, to_right, to_other = {"grid": left}, {"grid": right}, {"remap": other}
     greens = remote(gsend, gfar, to_left)
-    step = ri // SIBLING_CHUNKS
+    step = ri // P_CHUNKS
     siblings = [
         remote(tensor.at[0, pl.ds(i * step, step)], traw.at[core, pl.ds(i * step, step)], to_other)
-        for i in range(SIBLING_CHUNKS)
+        for i in range(P_CHUNKS)
     ]
     raws = [
         remote(rows.at[pl.ds(a, b - a)], far.at[pl.ds(a, b - a)], to_left)
         for a, b in zip(RAW_BOUNDS[:-1], RAW_BOUNDS[1:])
     ]
     firsts = [
-        remote(trans.at[0, pl.ds(a, b - a)], first.at[pl.ds(a - FIRST_BOUNDS[0], b - a)], to_right)
-        for a, b in zip(FIRST_BOUNDS[:-1], FIRST_BOUNDS[1:])
+        remote(
+            trans.at[0, pl.ds(FIRST_FROM, KEEP1), pl.ds(i * step, step)],
+            first.at[:, pl.ds(i * step, step)],
+            to_right,
+        )
+        for i in range(P_CHUNKS)
     ]
     seconds = [
         remote(trans.at[1, pl.ds(a, b - a)], second.at[pl.ds(a - SECOND_BOUNDS[0], b - a)], to_right)
         for a, b in zip(SECOND_BOUNDS[:-1], SECOND_BOUNDS[1:])
     ]
-    back_right = remote(part_right, ret_right, to_left)
-    back_left = remote(part_left, ret_left, to_right)
+    back_right = remote(back_right_send, ret_right, to_left)
+    back_left = remote(back_left_send, ret_left, to_right)
     finals = [remote(fin_send.at[d], fin_recv.at[d], to_other) for d in (RIGHT, LEFT, SELF)]
 
     def picked(ref, target):
@@ -94,11 +104,6 @@
     in_row = lax.broadcasted_iota(jnp.int32, (256, 256), 1)
     perm[...] = (in_row == (out_row & 15) * 16 + (out_row >> 4)).astype(F32).astype(BF)
 
-    pl.semaphore_wait(barrier, 3)
-    greens.start()
-    for copy in siblings:
-        copy.start()
-
     n_at = lax.broadcasted_iota(jnp.int32, (half, BS), 0) + core * half
     n_of = lax.broadcasted_iota(jnp.int32, (half, BS), 1)
     choose = (n_at == n_of).astype(F32).astype(BF)
@@ -113,8 +118,6 @@
 
     got2[0] = doubled(picked(gv_ref, right))
     got2[2] = doubled(picked(gv_ref, grid_at))
-
-    load.wait()
 
     def turn(n0):
         def body(i, carry):
@@ -129,12 +132,16 @@
 
         lax.fori_loop(0, ri // 32, body, 0)
 
-    sent = 0
-    for n0 in range(0, half, 16):
-        turn(n0)
-        while sent < len(raws) and RAW_BOUNDS[sent + 1] <= n0 + 16:
-            raws[sent].start()
-            sent += 1
+    loads[0].wait()
+    turn(0)
+
+    pl.semaphore_wait(barrier, 3)
+    greens.start()
+    for copy in siblings:
+        copy.start()
+    raws[0].start()
+    raws[1].start()
+    loads[1].wait()
 
     greens.wait_recv()
     green[pl.ds(half, half)] = nt(choose, gfar[1]).astype(BF)
@@ -151,11 +158,7 @@
             occ[p0 + j] = product[:, j * BS:(j + 1) * BS]
         return carry
 
-    for i in range(SIBLING_CHUNKS):
-        siblings[i].wait_recv()
-        lax.fori_loop(i * step // 8, (i + 1) * step // 8, first_product, 0)
-
-    def second_product(direction, n0):
+    def second_product(direction, n0, start, size):
         def body(i, carry):
             for u in range(2):
                 p0 = pl.multiple_of(i * 32 + u * 16, 16)
@@ -171,14 +174,19 @@
                     )
             return carry
 
-        lax.fori_loop(0, ri // 32, body, 0)
-
-    second_product(0, 32)
-    for copy in firsts:
-        copy.start()
-    second_product(1, 32)
-    for copy in seconds:
-        copy.start()
+        lax.fori_loop(start // 32, (start + size) // 32, body, 0)
+
+    for i in range(P_CHUNKS):
+        siblings[i].wait_recv()
+        lax.fori_loop(i * step // 8, (i + 1) * step // 8, first_product, 0)
+        second_product(0, 32, i * step, step)
+        firsts[i].start()
+    turn(16)
+    raws[2].start()
+    second_product(1, 32, 0, ri)
+    seconds[0].start()
+    turn(32)
+    turn(48)
 
     def wide(ref, at, many):
         return jnp.concatenate([ref[at + j] for j in range(many)], axis=1)
@@ -197,72 +205,82 @@
         if rest:
             acc[...] += nt(wide(x, x0 + 4 * groups, rest), wide(y, y0 + 4 * groups, rest))
 
-    second_product(0, 0)
-    second_product(1, 0)
+    second_product(0, 0, 0, ri)
+    second_product(1, 0, 0, ri)
+
+    theirs = pl.ds(pl.multiple_of(other * share, share), share)
+    mine = pl.ds(pl.multiple_of(core * share, share), share)
 
     def raw_chunk(i):
         a, b = RAW_BOUNDS[i], RAW_BOUNDS[i + 1]
         raws[i].wait_recv()
+        if i + 3 < len(raws):
+            raws[i + 3].start()
         contract(acc_right, trans.at[0], a, far, a, b - a, clear=i == 0)
         if b <= SECOND_BOUNDS[0]:
             contract(part_left, far, a, trans.at[1], a, b - a, clear=i == 0)
 
+    def second_chunk(i):
+        a, b = SECOND_BOUNDS[i], SECOND_BOUNDS[i + 1]
+        seconds[i].wait_recv()
+        contract(acc_left, rows, a, second, a - SECOND_BOUNDS[0], b - a, clear=i == 0)
+
     raw_chunk(0)
-    second_product(2, 32)
-    second_product(2, 0)
+    second_product(2, 32, 0, ri)
+    second_product(2, 0, 0, ri)
     raw_chunk(1)
     contract(acc_self, trans.at[2], 0, rows, 0, half, clear=True)
-    fin_send[SELF] = acc_self[pl.ds(pl.multiple_of(other * share, share), share), :]
+    fin_send[SELF] = acc_self[theirs, :]
     finals[SELF].start()
 
     raw_chunk(2)
+    for copy in firsts:
+        copy.wait_recv()
+    seconds[1].start()
+    contract(part_right, first, 0, rows, FIRST_FROM, KEEP1, clear=True)
+    back_right_send[...] = part_right[...].astype(BF)
+    back_right.start()
+    finals[SELF].wait_recv()
+    out_self[...] = acc_self[mine, :] + fin_recv[SELF]
     raw_chunk(3)
-    for i, copy in enumerate(firsts):
-        a, b = FIRST_BOUNDS[i], FIRST_BOUNDS[i + 1]
-        copy.wait_recv()
-        contract(part_right, first, a - FIRST_BOUNDS[0], rows, a, b - a, clear=i == 0)
-    back_right.start()
     raw_chunk(4)
+    second_chunk(0)
     raw_chunk(5)
+    back_left_send[...] = part_left[...].astype(BF)
     back_left.start()
     raw_chunk(6)
-    for i, copy in enumerate(seconds):
-        a, b = SECOND_BOUNDS[i], SECOND_BOUNDS[i + 1]
-        copy.wait_recv()
-        contract(acc_left, rows, a, second, a - SECOND_BOUNDS[0], b - a, clear=i == 0)
-
-    theirs = pl.ds(pl.multiple_of(other * share, share), share)
-    mine = pl.ds(pl.multiple_of(core * share, share), share)
+
     back_right.wait_recv()
-    fin_send[RIGHT] = acc_right[theirs, :] + ret_right[theirs, :]
+    fin_send[RIGHT] = acc_right[theirs, :] + ret_right[theirs, :].astype(F32)
     finals[RIGHT].start()
+    second_chunk(1)
     back_left.wait_recv()
-    fin_send[LEFT] = acc_left[theirs, :] + ret_left[theirs, :]
+    fin_send[LEFT] = acc_left[theirs, :] + ret_left[theirs, :].astype(F32)
     finals[LEFT].start()
-    finals[SELF].wait_recv()
-    out[SELF] = acc_self[mine, :] + fin_recv[SELF]
     finals[RIGHT].wait_recv()
-    out[RIGHT] = acc_right[mine, :] + ret_right[mine, :] + fin_recv[RIGHT]
+    out_right[...] = acc_right[mine, :] + ret_right[mine, :].astype(F32) + fin_recv[RIGHT]
     finals[LEFT].wait_recv()
-    out[LEFT] = acc_left[mine, :] + ret_left[mine, :] + fin_recv[LEFT]
+    out_left[...] = acc_left[mine, :] + ret_left[mine, :].astype(F32) + fin_recv[LEFT]
 
     for copy in [greens, *siblings, *raws, *firsts, *seconds, back_right, back_left, *finals]:
         copy.wait_send()
 
 
-COPIES = 1 + SIBLING_CHUNKS + len(RAW_BOUNDS) + len(FIRST_BOUNDS) + len(SECOND_BOUNDS) - 3 + 2 + 3
+COPIES = 1 + 2 * P_CHUNKS + len(RAW_BOUNDS) + len(SECOND_BOUNDS) - 2 + 2 + 3
 
 
 def on_device(tensor, go_blocks, gv_blocks, partners):
     _, ri, half, _ = tensor.shape
     share = ri // 2
     square = pltpu.VMEM((ri, ri), F32)
+    narrow = pltpu.VMEM((ri, ri), BF)
     vmem = pl.BlockSpec(memory_space=pltpu.VMEM)
-    parts = pl.pallas_call(
+    result = jax.ShapeDtypeStruct((share, ri), F32)
+    to_right, to_left, to_self = pl.pallas_call(
         kernel,
-        out_shape=jax.ShapeDtypeStruct((3, share, ri), F32),
+        out_shape=[result] * 3,
         in_specs=[pl.BlockSpec(memory_space=pl.ANY), vmem, vmem, pl.BlockSpec(memory_space=pltpu.SMEM)],
-        out_specs=vmem,
+        out_specs=[vmem] * 3,
         scratch_shapes=[
             pltpu.VMEM((2, ri, half, BS), BF),
             pltpu.VMEM((half, ri, BS), BF),
@@ -276,10 +294,11 @@
             pltpu.VMEM((2, BS, BS), BF),
             pltpu.VMEM((KEEP1, ri, BS), BF),
             pltpu.VMEM((KEEP2, ri, BS), BF),
-            square, square, square, square, square, square, square,
+            square, square, square, square, square,
+            narrow, narrow, narrow, narrow,
             pltpu.VMEM((3, share, ri), F32),
             pltpu.VMEM((3, share, ri), F32),
-            pltpu.SemaphoreType.DMA,
+            pltpu.SemaphoreType.DMA((2,)),
             pltpu.SemaphoreType.DMA((COPIES,)),
             pltpu.SemaphoreType.DMA((COPIES,)),
         ],
@@ -292,8 +311,8 @@
     where_to = partners[0][:, None, None]
     chosen = jnp.where(
         where_to == lax.rem(grid_at + 1, count),
-        parts[RIGHT][None],
-        jnp.where(where_to == grid_at, parts[SELF][None], parts[LEFT][None]),
+        to_right[None],
+        jnp.where(where_to == grid_at, to_self[None], to_left[None]),
     )
     return chosen[None]
 

time: 102 us -> 96.1 us (0.942)
  Pallas kernels: 99.6 us -> 93.4 us
  other arithmetic: 0.8 us -> 2.49 us
  local copies, waits for them, and re-layouts: 1.06 us -> 0 us
    pallas_call x1, Pallas kernels: 99.6 us -> 93.4 us  [on_device(): pl.pallas_call(kernel, out_shape=[result] * 3, in_specs=[pl.BlockSpec(mem...]
    broadcast_in_dim x1 -> x0, local copies, waits for them, and re-layouts: 1.06 us -> none  [on_device(): jnp.where(where_to == lax.rem(grid_at + 1, count), parts[RIGHT][None], jn...]
    select_n x1, other arithmetic: 0.8 us -> 1.83 us  [on_device(): jnp.where(where_to == lax.rem(grid_at + 1, count), to_right[None], jnp.wh...]
where the time goes in v2:
time: 96.1 us; the launch traced here: 95.9 us
  Pallas kernels  93.4 us (97%)
  other arithmetic  2.49 us (3%)
    pallas_call x1, Pallas kernels, on_device(): pl.pallas_call(kernel, out_shape=[result] * 3, in_specs=[pl.BlockSpec(mem...  93.4 us

profile of v2, /device:TPU:1, one launch (start us, length us, event | category | flops | bytes accessed | tf_op | source)
XLA Modules:
  0.0 95.9 jit_solution(7349451719745957516)
XLA Ops:
  0.0 0.7 compare_bitcast_fusion.1
  0.7 93.4 %shard_map.46 = (f32[128,256]{1,0:T(8,128)}, f32[128,256]{1,0:T(8,128)}, f32[128,256]{1,0:T(8,128)}) custom-call(bf16[1,256,64,128]{3,2,1,0:T(8,128)(2,1)} %tensor.1, bf16[1,2,128,128]{3,2,1,0:T(8,128)(2,1)} %go_ref.1, bf16[1,2,128,128]{3,2,1,0:T(8,128)(2,1)} %gv_ref.1, s32[1,2]{1,0:T(1,128)} %partners.1), custom_call_target="tpu_custom_call" | custom-call | tf_op jit(solution)/shard_map/pallas_call | solution.py:279
  94.1 1.8 %select_select_fusion = f32[1,2,128,256]{3,2,1,0:T(8,128)} fusion(f32[128,256]{1,0:T(8,128)} %get-tuple-element.10, f32[128,256]{1,0:T(8,128)} %get-tuple-element.9, f32[128,256]{1,0:T(8,128)} %get-tuple-element.8, pred[2]{0:T(512)(128)(4,1)S(1)} %get-tuple-element.12, pred[2]{0:T(512)(128)(4,1)S(1)} %get-tuple-element.11), kind=kLoop, calls=%fused_computation | loop fusion | flops 131072 | bytes 655364 | tf_op jit(solution)/shard_map/jit(_where)/select_n | solution.py:312

commit v3 on v2

--- a/solution.py
+++ b/solution.py
@@ -11,11 +11,12 @@
 BS = 128
 
 KEEP1 = 20
-KEEP2 = 22
-RAW_BOUNDS = (0, 8, 16, 24, 32, 38, 42, 44)
+KEEP2 = 23
+RAW_BOUNDS = (0, 8, 16, 24, 32, 37, 41, 44)
 FIRST_FROM = 64 - KEEP1
-SECOND_BOUNDS = (42, 54, 64)
-P_CHUNKS = 4
+SECOND_BOUNDS = (41, 53, 64)
+P_BOUNDS = (0, 32, 64, 128, 256)
+P_CHUNKS = len(P_BOUNDS) - 1
 
 RIGHT, LEFT, SELF = 0, 1, 2
 
@@ -25,10 +26,10 @@
 
 
 def kernel(
-    tensor, go_ref, gv_ref, partners, out_right, out_left, out_self,
-    traw, rows, far, occ, trans, got2, perm, green, gsend, gfar, first, second,
+    tensor, go_hbm, gv_hbm, partners, out,
+    traw, rows, far, occ, trans, got2, perm, green, go_ref, gv_ref, gsend, gfar, first, second,
     acc_right, acc_left, acc_self, part_right, part_left,
-    back_right_send, back_left_send, ret_right, ret_left,
+    half_send, half_recv, back_right_send, back_left_send, ret_right, ret_left,
     fin_send, fin_recv, load_sem, send_sem, recv_sem,
 ):
     half = rows.shape[0]
@@ -41,17 +42,21 @@
     left = lax.rem(grid_at + count - 1, count)
     other = 1 - core
 
+    barrier = pltpu.get_barrier_semaphore()
+    for target in ({"grid": left}, {"grid": right}, {"remap": other}):
+        pl.semaphore_signal(barrier, inc=1, device_id=target, device_id_type=MESH)
+
     def loaded(at, n0, size):
         span = pl.ds(n0, size)
         return pltpu.make_async_copy(tensor.at[0, :, span], traw.at[core, :, span], load_sem.at[at])
 
     loads = [loaded(0, 0, 16), loaded(1, 16, half - 16)]
-    for copy in loads:
+    loads += [
+        pltpu.make_async_copy(go_hbm.at[0], go_ref, load_sem.at[2]),
+        pltpu.make_async_copy(gv_hbm.at[0], gv_ref, load_sem.at[3]),
+    ]
+    for copy in loads[2:] + loads[:2]:
         copy.start()
-
-    barrier = pltpu.get_barrier_semaphore()
-    for target in ({"grid": left}, {"grid": right}, {"remap": other}):
-        pl.semaphore_signal(barrier, inc=1, device_id=target, device_id_type=MESH)
 
     used = [0]
 
@@ -65,22 +70,20 @@
 
     to_left, to_right, to_other = {"grid": left}, {"grid": right}, {"remap": other}
     greens = remote(gsend, gfar, to_left)
-    step = ri // P_CHUNKS
+    theirs = pl.ds(pl.multiple_of(other * share, share), share)
+    mine = pl.ds(pl.multiple_of(core * share, share), share)
+    p_spans = [pl.ds(a, b - a) for a, b in zip(P_BOUNDS[:-1], P_BOUNDS[1:])]
     siblings = [
-        remote(tensor.at[0, pl.ds(i * step, step)], traw.at[core, pl.ds(i * step, step)], to_other)
-        for i in range(P_CHUNKS)
+        remote(tensor.at[0, span], traw.at[core, span], to_other)
+        for span in p_spans
     ]
     raws = [
         remote(rows.at[pl.ds(a, b - a)], far.at[pl.ds(a, b - a)], to_left)
         for a, b in zip(RAW_BOUNDS[:-1], RAW_BOUNDS[1:])
     ]
     firsts = [
-        remote(
-            trans.at[0, pl.ds(FIRST_FROM, KEEP1), pl.ds(i * step, step)],
-            first.at[:, pl.ds(i * step, step)],
-            to_right,
-        )
-        for i in range(P_CHUNKS)
+        remote(trans.at[0, pl.ds(FIRST_FROM, KEEP1), span], first.at[:, span], to_right)
+        for span in p_spans
     ]
     seconds = [
         remote(trans.at[1, pl.ds(a, b - a)], second.at[pl.ds(a - SECOND_BOUNDS[0], b - a)], to_right)
@@ -88,17 +91,15 @@
     ]
     back_right = remote(back_right_send, ret_right, to_left)
     back_left = remote(back_left_send, ret_left, to_right)
+    halves = [remote(half_send.at[d], half_recv.at[d], to_other) for d in (RIGHT, LEFT)]
     finals = [remote(fin_send.at[d], fin_recv.at[d], to_other) for d in (RIGHT, LEFT, SELF)]
 
     def picked(ref, target):
         total = jnp.zeros((BS, BS), F32)
         for slot in range(2):
             weight = (partners[0, slot] == target).astype(F32)
-            total = total + ref[0, slot].astype(F32) * weight
+            total = total + ref[slot].astype(F32) * weight
         return total.astype(BF)
-
-    gsend[0] = picked(go_ref, left)
-    gsend[1] = picked(gv_ref, left)
 
     out_row = lax.broadcasted_iota(jnp.int32, (256, 256), 0)
     in_row = lax.broadcasted_iota(jnp.int32, (256, 256), 1)
@@ -107,6 +108,10 @@
     n_at = lax.broadcasted_iota(jnp.int32, (half, BS), 0) + core * half
     n_of = lax.broadcasted_iota(jnp.int32, (half, BS), 1)
     choose = (n_at == n_of).astype(F32).astype(BF)
+    loads[2].wait()
+    loads[3].wait()
+    gsend[pl.ds(0, BS)] = picked(go_ref, left)
+    gsend[pl.ds(BS, half)] = nt(choose, picked(gv_ref, left)).astype(BF)
     green[pl.ds(0, half)] = nt(choose, picked(go_ref, right)).astype(BF)
     green[pl.ds(2 * half, half)] = nt(choose, picked(go_ref, grid_at)).astype(BF)
     empty = jnp.zeros((BS, BS), BF)
@@ -144,8 +149,8 @@
     loads[1].wait()
 
     greens.wait_recv()
-    green[pl.ds(half, half)] = nt(choose, gfar[1]).astype(BF)
-    got2[1] = doubled(gfar[0])
+    green[pl.ds(half, half)] = gfar[pl.ds(BS, half)]
+    got2[1] = doubled(gfar[pl.ds(0, BS)])
 
     def first_product(i, carry):
         p0 = pl.multiple_of(i * 8, 8)
@@ -178,8 +183,9 @@
 
     for i in range(P_CHUNKS):
         siblings[i].wait_recv()
-        lax.fori_loop(i * step // 8, (i + 1) * step // 8, first_product, 0)
-        second_product(0, 32, i * step, step)
+        a, b = P_BOUNDS[i], P_BOUNDS[i + 1]
+        lax.fori_loop(a // 8, b // 8, first_product, 0)
+        second_product(0, 32, a, b - a)
         firsts[i].start()
     turn(16)
     raws[2].start()
@@ -208,8 +214,19 @@
     second_product(0, 0, 0, ri)
     second_product(1, 0, 0, ri)
 
-    theirs = pl.ds(pl.multiple_of(other * share, share), share)
-    mine = pl.ds(pl.multiple_of(core * share, share), share)
+    def swap_halves(direction, part):
+        half_send[direction] = part[theirs, :]
+        halves[direction].start()
+
+    def send_back(direction, part, narrow, copy):
+        halves[direction].wait_recv()
+        narrow[...] = (part[mine, :] + half_recv[direction]).astype(BF)
+        copy.start()
+
+    def put(target, total, clear=False):
+        for slot in range(2):
+            term = total * (partners[0, slot] == target).astype(F32)
+            out[slot] = term if clear else out[slot] + term
 
     def raw_chunk(i):
         a, b = RAW_BOUNDS[i], RAW_BOUNDS[i + 1]
@@ -238,49 +255,49 @@
         copy.wait_recv()
     seconds[1].start()
     contract(part_right, first, 0, rows, FIRST_FROM, KEEP1, clear=True)
-    back_right_send[...] = part_right[...].astype(BF)
-    back_right.start()
+    swap_halves(RIGHT, part_right)
     finals[SELF].wait_recv()
-    out_self[...] = acc_self[mine, :] + fin_recv[SELF]
+    put(grid_at, acc_self[mine, :] + fin_recv[SELF], clear=True)
+    send_back(RIGHT, part_right, back_right_send, back_right)
     raw_chunk(3)
     raw_chunk(4)
     second_chunk(0)
     raw_chunk(5)
-    back_left_send[...] = part_left[...].astype(BF)
-    back_left.start()
+    swap_halves(LEFT, part_left)
+    send_back(LEFT, part_left, back_left_send, back_left)
     raw_chunk(6)
 
-    back_right.wait_recv()
-    fin_send[RIGHT] = acc_right[theirs, :] + ret_right[theirs, :].astype(F32)
+    fin_send[RIGHT] = acc_right[theirs, :]
     finals[RIGHT].start()
     second_chunk(1)
+    fin_send[LEFT] = acc_left[theirs, :]
+    finals[LEFT].start()
+    back_right.wait_recv()
+    finals[RIGHT].wait_recv()
+    put(right, acc_right[mine, :] + ret_right[...].astype(F32) + fin_recv[RIGHT])
     back_left.wait_recv()
-    fin_send[LEFT] = acc_left[theirs, :] + ret_left[theirs, :].astype(F32)
-    finals[LEFT].start()
-    finals[RIGHT].wait_recv()
-    out_right[...] = acc_right[mine, :] + ret_right[mine, :].astype(F32) + fin_recv[RIGHT]
     finals[LEFT].wait_recv()
-    out_left[...] = acc_left[mine, :] + ret_left[mine, :].astype(F32) + fin_recv[LEFT]
-
-    for copy in [greens, *siblings, *raws, *firsts, *seconds, back_right, back_left, *finals]:
+    put(left, acc_left[mine, :] + ret_left[...].astype(F32) + fin_recv[LEFT])
+
+    for copy in [greens, *siblings, *raws, *firsts, *seconds, *halves, back_right, back_left, *finals]:
         copy.wait_send()
 
 
-COPIES = 1 + 2 * P_CHUNKS + len(RAW_BOUNDS) + len(SECOND_BOUNDS) - 2 + 2 + 3
+COPIES = 1 + 2 * P_CHUNKS + len(RAW_BOUNDS) + len(SECOND_BOUNDS) - 2 + 4 + 3
 
 
 def on_device(tensor, go_blocks, gv_blocks, partners):
     _, ri, half, _ = tensor.shape
     share = ri // 2
     square = pltpu.VMEM((ri, ri), F32)
-    narrow = pltpu.VMEM((ri, ri), BF)
-    vmem = pl.BlockSpec(memory_space=pltpu.VMEM)
-    result = jax.ShapeDtypeStruct((share, ri), F32)
-    to_right, to_left, to_self = pl.pallas_call(
+    narrow = pltpu.VMEM((share, ri), BF)
+    blocks = pltpu.VMEM((2, BS, BS), BF)
+    green_rows = pltpu.VMEM((BS + half, BS), BF)
+    result = pl.pallas_call(
         kernel,
-        out_shape=[result] * 3,
-        in_specs=[pl.BlockSpec(memory_space=pl.ANY), vmem, vmem, pl.BlockSpec(memory_space=pltpu.SMEM)],
-        out_specs=[vmem] * 3,
+        out_shape=jax.ShapeDtypeStruct((2, share, ri), F32),
+        in_specs=[pl.BlockSpec(memory_space=pl.ANY)] * 3 + [pl.BlockSpec(memory_space=pltpu.SMEM)],
+        out_specs=pl.BlockSpec(memory_space=pltpu.VMEM),
         scratch_shapes=[
             pltpu.VMEM((2, ri, half, BS), BF),
             pltpu.VMEM((half, ri, BS), BF),
@@ -290,15 +307,16 @@
             pltpu.VMEM((3, 2 * BS, 2 * BS), BF),
             pltpu.VMEM((256, 256), BF),
             pltpu.VMEM((3 * half, BS), BF),
-            pltpu.VMEM((2, BS, BS), BF),
-            pltpu.VMEM((2, BS, BS), BF),
+            blocks, blocks, green_rows, green_rows,
             pltpu.VMEM((KEEP1, ri, BS), BF),
             pltpu.VMEM((KEEP2, ri, BS), BF),
             square, square, square, square, square,
+            pltpu.VMEM((2, share, ri), F32),
+            pltpu.VMEM((2, share, ri), F32),
             narrow, narrow, narrow, narrow,
             pltpu.VMEM((3, share, ri), F32),
             pltpu.VMEM((3, share, ri), F32),
-            pltpu.SemaphoreType.DMA((2,)),
+            pltpu.SemaphoreType.DMA((4,)),
             pltpu.SemaphoreType.DMA((COPIES,)),
             pltpu.SemaphoreType.DMA((COPIES,)),
         ],
@@ -306,15 +324,7 @@
             collective_id=0, has_side_effects=True, vmem_limit_bytes=58 * 1024 * 1024
         ),
     )(tensor, go_blocks, gv_blocks, partners)
-    count = lax.axis_size("grid")
-    grid_at = lax.axis_index("grid")
-    where_to = partners[0][:, None, None]
-    chosen = jnp.where(
-        where_to == lax.rem(grid_at + 1, count),
-        to_right[None],
-        jnp.where(where_to == grid_at, to_self[None], to_left[None]),
-    )
-    return chosen[None]
+    return result[None]
 
 
 def solution(mesh):

time: 96.1 us -> 93.2 us (0.970)
  other arithmetic: 2.49 us -> 0 us
  Pallas kernels: 93.4 us -> 91.4 us
  local copies, waits for them, and re-layouts: 0 us -> 1.67 us
    pallas_call x1, Pallas kernels: 93.4 us -> 91.4 us  [on_device(): pl.pallas_call(kernel, out_shape=jax.ShapeDtypeStruct((2, share, ri), F32...]
    select_n x1 -> x0, other arithmetic: 1.83 us -> none  [on_device(): jnp.where(where_to == lax.rem(grid_at + 1, count), to_right[None], jnp.wh...]
    unnamed x0 -> x1, local copies, waits for them, and re-layouts: none -> 1.67 us
where the time goes in v3:
time: 93.2 us; the launch traced here: 93.1 us
  Pallas kernels  91.4 us (98%)
  local copies, waits for them, and re-layouts  1.67 us (2%)
    pallas_call x1, Pallas kernels, on_device(): pl.pallas_call(kernel, out_shape=jax.ShapeDtypeStruct((2, share, ri), F32...  91.4 us

profile of v3, /device:TPU:1, one launch (start us, length us, event | category | flops | bytes accessed | tf_op | source)
XLA Modules:
  0.0 93.1 jit_solution(9747754876236302877)
XLA Ops:
  0.0 91.4 %shard_map.46 = f32[2,128,256]{2,1,0:T(8,128)} custom-call(bf16[1,256,64,128]{3,2,1,0:T(8,128)(2,1)} %tensor.1, bf16[1,2,128,128]{3,2,1,0:T(8,128)(2,1)} %go_hbm.1, bf16[1,2,128,128]{3,2,1,0:T(8,128)(2,1)} %gv_hbm.1, s32[1,2]{1,0:T(1,128)} %partners.1), custom_call_target="tpu_custom_call" | custom-call | tf_op jit(solution)/shard_map/pallas_call | solution.py:296
  91.4 1.7 %copy.6 = f32[1,2,128,256]{3,2,1,0:T(8,128)} copy(f32[1,2,128,256]{3,2,1,0:T(8,128)} %bitcast.1) | data formatting | bytes 524288

commit v4 on v3

--- a/solution.py
+++ b/solution.py
@@ -14,7 +14,7 @@
 KEEP2 = 23
 RAW_BOUNDS = (0, 8, 16, 24, 32, 37, 41, 44)
 FIRST_FROM = 64 - KEEP1
-SECOND_BOUNDS = (41, 53, 64)
+SECOND_BOUNDS = (41, 51, 59, 64)
 P_BOUNDS = (0, 32, 64, 128, 256)
 P_CHUNKS = len(P_BOUNDS) - 1
 
@@ -124,21 +124,29 @@
     got2[0] = doubled(picked(gv_ref, right))
     got2[2] = doubled(picked(gv_ref, grid_at))
 
-    def turn(n0):
+    def turn(n_blocks):
+        width = 64 if len(n_blocks) == 1 else 32
+
         def body(i, carry):
-            q0 = pl.multiple_of(i * 32, 32)
-            pair = [
-                traw[core, pl.ds(q0 + 16 * j, 16), pl.ds(n0, 16), :].reshape(256, BS) for j in range(2)
-            ]
-            turned = jnp.dot(perm[...], jnp.concatenate(pair, axis=1), preferred_element_type=F32).astype(BF)
-            for j in range(2):
-                rows[pl.ds(n0, 16), pl.ds(q0 + 16 * j, 16), :] = turned[:, j * BS:(j + 1) * BS].reshape(16, 16, BS)
+            for n0 in n_blocks:
+                for u in range(width // 32):
+                    q0 = pl.multiple_of(i * width + u * 32, 32)
+                    pair = [
+                        traw[core, pl.ds(q0 + 16 * j, 16), pl.ds(n0, 16), :].reshape(256, BS) for j in range(2)
+                    ]
+                    turned = jnp.dot(
+                        perm[...], jnp.concatenate(pair, axis=1), preferred_element_type=F32
+                    ).astype(BF)
+                    for j in range(2):
+                        rows[pl.ds(n0, 16), pl.ds(q0 + 16 * j, 16), :] = (
+                            turned[:, j * BS:(j + 1) * BS].reshape(16, 16, BS)
+                        )
             return carry
 
-        lax.fori_loop(0, ri // 32, body, 0)
+        lax.fori_loop(0, ri // width, body, 0)
 
     loads[0].wait()
-    turn(0)
+    turn([0])
 
     pl.semaphore_wait(barrier, 3)
     greens.start()
@@ -163,56 +171,68 @@
             occ[p0 + j] = product[:, j * BS:(j + 1) * BS]
         return carry
 
-    def second_product(direction, n0, start, size):
+    def second_product(parts, start, size):
+        width = 32 if len(parts) > 1 or size == 32 else 64
+
         def body(i, carry):
-            for u in range(2):
-                p0 = pl.multiple_of(i * 32 + u * 16, 16)
-                pair = [
-                    occ[pl.ds(p0, 16), pl.ds(direction * half + n0 + 16 * j, 16), :].reshape(256, BS)
-                    for j in range(2)
-                ]
-                turned = jnp.dot(perm[...], jnp.concatenate(pair, axis=1), preferred_element_type=F32).astype(BF)
-                product = nt(turned, got2[direction]).astype(BF)
-                for j in range(2):
-                    trans[direction, pl.ds(n0 + 16 * j, 16), pl.ds(p0, 16), :] = (
-                        product[:, j * BS:(j + 1) * BS].reshape(16, 16, BS)
-                    )
+            for direction, n0 in parts:
+                for u in range(width // 16):
+                    p0 = pl.multiple_of(i * width + u * 16, 16)
+                    pair = [
+                        occ[pl.ds(p0, 16), pl.ds(direction * half + n0 + 16 * j, 16), :].reshape(256, BS)
+                        for j in range(2)
+                    ]
+                    turned = jnp.dot(
+                        perm[...], jnp.concatenate(pair, axis=1), preferred_element_type=F32
+                    ).astype(BF)
+                    product = nt(turned, got2[direction]).astype(BF)
+                    for j in range(2):
+                        trans[direction, pl.ds(n0 + 16 * j, 16), pl.ds(p0, 16), :] = (
+                            product[:, j * BS:(j + 1) * BS].reshape(16, 16, BS)
+                        )
             return carry
 
-        lax.fori_loop(start // 32, (start + size) // 32, body, 0)
+        lax.fori_loop(start // width, (start + size) // width, body, 0)
 
     for i in range(P_CHUNKS):
         siblings[i].wait_recv()
         a, b = P_BOUNDS[i], P_BOUNDS[i + 1]
         lax.fori_loop(a // 8, b // 8, first_product, 0)
-        second_product(0, 32, a, b - a)
+        second_product([(0, 32)], a, b - a)
         firsts[i].start()
-    turn(16)
+    turn([16])
     raws[2].start()
-    second_product(1, 32, 0, ri)
+    second_product([(1, 32)], 0, ri)
     seconds[0].start()
-    turn(32)
-    turn(48)
+    turn([32, 48])
+    raws[3].start()
+    raws[4].start()
 
     def wide(ref, at, many):
         return jnp.concatenate([ref[at + j] for j in range(many)], axis=1)
 
-    def contract(acc, x, x0, y, y0, size, clear=False):
+    def contract(jobs, size, clear=False):
         if clear:
-            acc[...] = jnp.zeros_like(acc)
-        groups, rest = divmod(size, 4)
+            for acc, *_ in jobs:
+                acc[...] = jnp.zeros_like(acc)
+        groups, rest = divmod(size, 8)
+
+        def add(at, many):
+            for acc, x, x0, y, y0 in jobs:
+                acc[...] += nt(wide(x, x0 + at, many), wide(y, y0 + at, many))
 
         def body(i, carry):
-            acc[...] += nt(wide(x, x0 + 4 * i, 4), wide(y, y0 + 4 * i, 4))
+            add(8 * i, 8)
             return carry
 
-        if groups:
+        if groups > 1:
             lax.fori_loop(0, groups, body, 0)
+        elif groups:
+            add(0, 8)
         if rest:
-            acc[...] += nt(wide(x, x0 + 4 * groups, rest), wide(y, y0 + 4 * groups, rest))
-
-    second_product(0, 0, 0, ri)
-    second_product(1, 0, 0, ri)
+            add(8 * groups, rest)
+
+    second_product([(0, 0), (1, 0)], 0, ri)
 
     def swap_halves(direction, part):
         half_send[direction] = part[theirs, :]
@@ -231,30 +251,31 @@
     def raw_chunk(i):
         a, b = RAW_BOUNDS[i], RAW_BOUNDS[i + 1]
         raws[i].wait_recv()
-        if i + 3 < len(raws):
-            raws[i + 3].start()
-        contract(acc_right, trans.at[0], a, far, a, b - a, clear=i == 0)
+        jobs = [(acc_right, trans.at[0], a, far, a)]
         if b <= SECOND_BOUNDS[0]:
-            contract(part_left, far, a, trans.at[1], a, b - a, clear=i == 0)
+            jobs.append((part_left, far, a, trans.at[1], a))
+        contract(jobs, b - a, clear=i == 0)
 
     def second_chunk(i):
         a, b = SECOND_BOUNDS[i], SECOND_BOUNDS[i + 1]
         seconds[i].wait_recv()
-        contract(acc_left, rows, a, second, a - SECOND_BOUNDS[0], b - a, clear=i == 0)
+        contract([(acc_left, rows, a, second, a - SECOND_BOUNDS[0])], b - a, clear=i == 0)
 
     raw_chunk(0)
-    second_product(2, 32, 0, ri)
-    second_product(2, 0, 0, ri)
+    raws[5].start()
+    seconds[1].start()
+    second_product([(2, 32), (2, 0)], 0, ri)
     raw_chunk(1)
-    contract(acc_self, trans.at[2], 0, rows, 0, half, clear=True)
+    raws[6].start()
+    seconds[2].start()
+    contract([(acc_self, trans.at[2], 0, rows, 0)], half, clear=True)
     fin_send[SELF] = acc_self[theirs, :]
     finals[SELF].start()
 
     raw_chunk(2)
     for copy in firsts:
         copy.wait_recv()
-    seconds[1].start()
-    contract(part_right, first, 0, rows, FIRST_FROM, KEEP1, clear=True)
+    contract([(part_right, first, 0, rows, FIRST_FROM)], KEEP1, clear=True)
     swap_halves(RIGHT, part_right)
     finals[SELF].wait_recv()
     put(grid_at, acc_self[mine, :] + fin_recv[SELF], clear=True)
@@ -264,12 +285,13 @@
     second_chunk(0)
     raw_chunk(5)
     swap_halves(LEFT, part_left)
+    second_chunk(1)
     send_back(LEFT, part_left, back_left_send, back_left)
     raw_chunk(6)
 
     fin_send[RIGHT] = acc_right[theirs, :]
     finals[RIGHT].start()
-    second_chunk(1)
+    second_chunk(2)
     fin_send[LEFT] = acc_left[theirs, :]
     finals[LEFT].start()
     back_right.wait_recv()
@@ -321,7 +343,7 @@
             pltpu.SemaphoreType.DMA((COPIES,)),
         ],
         compiler_params=pltpu.CompilerParams(
-            collective_id=0, has_side_effects=True, vmem_limit_bytes=58 * 1024 * 1024
+            collective_id=0, has_side_effects=True, vmem_limit_bytes=52 * 1024 * 1024
         ),
     )(tensor, go_blocks, gv_blocks, partners)
     return result[None]

time: 93.2 us -> 93.6 us (level)
  local copies, waits for them, and re-layouts: 1.67 us -> 3.04 us
  Pallas kernels: 91.4 us -> 90.3 us
    unnamed x1 -> x7, local copies, waits for them, and re-layouts: 1.67 us -> 3.04 us
    pallas_call x1, Pallas kernels: 91.4 us -> 90.3 us  [on_device(): pl.pallas_call(kernel, out_shape=jax.ShapeDtypeStruct((2, share, ri), F32...]
where the time goes in v4:
time: 93.6 us; the launch traced here: 93.4 us
  Pallas kernels  90.3 us (96%)
  local copies, waits for them, and re-layouts  3.04 us (3%)
    pallas_call x1, Pallas kernels, on_device(): pl.pallas_call(kernel, out_shape=jax.ShapeDtypeStruct((2, share, ri), F32...  90.3 us
    unnamed x7, local copies, waits for them, and re-layouts  3.04 us

profile of v4, /device:TPU:1, one launch (start us, length us, event | category | flops | bytes accessed | tf_op | source)
XLA Modules:
  0.0 93.4 jit_solution(14812195396740951031)
XLA Ops:
  0.0 0.0 copy-start
  0.0 0.8 copy-done
  0.8 0.0 copy-start.1
  0.8 0.8 copy-done.1
  1.7 0.0 copy-start.2
  1.7 0.7 copy-done.2
  2.3 90.3 %shard_map.46 = f32[2,128,256]{2,1,0:T(8,128)S(1)} custom-call(bf16[1,256,64,128]{3,2,1,0:T(8,128)(2,1)} %tensor.1, bf16[1,2,128,128]{3,2,1,0:T(8,128)(2,1)S(1)} %copy-done, bf16[1,2,128,128]{3,2,1,0:T(8,128)(2,1)S(1)} %copy-done.1, s32[1,2]{1,0:T(1,128)S(1)} %copy-done.2), custom_call_target="tpu_custom_call" | custom-call | tf_op jit(solution)/shard_map/pallas_call | solution.py:318
  92.7 0.7 copy.6
Async XLA Ops:
  0.0 0.8 copy-start
  0.8 0.8 copy-start.1
  1.7 0.7 copy-start.2

commit v5 on v4

--- a/solution.py
+++ b/solution.py
@@ -11,10 +11,10 @@
 BS = 128
 
 KEEP1 = 20
-KEEP2 = 23
-RAW_BOUNDS = (0, 8, 16, 24, 32, 37, 41, 44)
+KEEP2 = 22
+RAW_BOUNDS = (0, 8, 16, 24, 32, 38, 42, 44)
 FIRST_FROM = 64 - KEEP1
-SECOND_BOUNDS = (41, 51, 59, 64)
+SECOND_BOUNDS = (42, 52, 60, 64)
 P_BOUNDS = (0, 32, 64, 128, 256)
 P_CHUNKS = len(P_BOUNDS) - 1
 
@@ -26,8 +26,8 @@
 
 
 def kernel(
-    tensor, go_hbm, gv_hbm, partners, out,
-    traw, rows, far, occ, trans, got2, perm, green, go_ref, gv_ref, gsend, gfar, first, second,
+    tensor, go_hbm, gv_hbm, partners_hbm, out,
+    traw, rows, far, occ, trans, got2, perm, green, partners, go_ref, gv_ref, gsend, gfar, first, second,
     acc_right, acc_left, acc_self, part_right, part_left,
     half_send, half_recv, back_right_send, back_left_send, ret_right, ret_left,
     fin_send, fin_recv, load_sem, send_sem, recv_sem,
@@ -52,8 +52,9 @@
 
     loads = [loaded(0, 0, 16), loaded(1, 16, half - 16)]
     loads += [
-        pltpu.make_async_copy(go_hbm.at[0], go_ref, load_sem.at[2]),
-        pltpu.make_async_copy(gv_hbm.at[0], gv_ref, load_sem.at[3]),
+        pltpu.make_async_copy(partners_hbm, partners, load_sem.at[2]),
+        pltpu.make_async_copy(go_hbm.at[0], go_ref, load_sem.at[3]),
+        pltpu.make_async_copy(gv_hbm.at[0], gv_ref, load_sem.at[4]),
     ]
     for copy in loads[2:] + loads[:2]:
         copy.start()
@@ -108,8 +109,8 @@
     n_at = lax.broadcasted_iota(jnp.int32, (half, BS), 0) + core * half
     n_of = lax.broadcasted_iota(jnp.int32, (half, BS), 1)
     choose = (n_at == n_of).astype(F32).astype(BF)
-    loads[2].wait()
-    loads[3].wait()
+    for copy in loads[2:]:
+        copy.wait()
     gsend[pl.ds(0, BS)] = picked(go_ref, left)
     gsend[pl.ds(BS, half)] = nt(choose, picked(gv_ref, left)).astype(BF)
     green[pl.ds(0, half)] = nt(choose, picked(go_ref, right)).astype(BF)
@@ -150,9 +151,10 @@
 
     pl.semaphore_wait(barrier, 3)
     greens.start()
-    for copy in siblings:
+    siblings[0].start()
+    raws[0].start()
+    for copy in siblings[1:]:
         copy.start()
-    raws[0].start()
     raws[1].start()
     loads[1].wait()
 
@@ -287,13 +289,22 @@
     swap_halves(LEFT, part_left)
     second_chunk(1)
     send_back(LEFT, part_left, back_left_send, back_left)
-    raw_chunk(6)
-
-    fin_send[RIGHT] = acc_right[theirs, :]
+    def last(x, x0, y, y0, many, span):
+        left_side = jnp.concatenate([x[x0 + j, span, :] for j in range(many)], axis=1)
+        return nt(left_side, wide(y, y0, many))
+
+    a, b = RAW_BOUNDS[-2], RAW_BOUNDS[-1]
+    right_end = (trans.at[0], a, far, a, b - a)
+    raws[-1].wait_recv()
+    fin_send[RIGHT] = acc_right[theirs, :] + last(*right_end, theirs)
     finals[RIGHT].start()
-    second_chunk(2)
-    fin_send[LEFT] = acc_left[theirs, :]
+    a, b = SECOND_BOUNDS[-2], SECOND_BOUNDS[-1]
+    left_end = (rows, a, second, a - SECOND_BOUNDS[0], b - a)
+    seconds[-1].wait_recv()
+    fin_send[LEFT] = acc_left[theirs, :] + last(*left_end, theirs)
     finals[LEFT].start()
+    acc_right[mine, :] += last(*right_end, mine)
+    acc_left[mine, :] += last(*left_end, mine)
     back_right.wait_recv()
     finals[RIGHT].wait_recv()
     put(right, acc_right[mine, :] + ret_right[...].astype(F32) + fin_recv[RIGHT])
@@ -312,13 +323,15 @@
     _, ri, half, _ = tensor.shape
     share = ri // 2
     square = pltpu.VMEM((ri, ri), F32)
+    operands = (tensor, go_blocks, gv_blocks, partners)
+    placed = [pltpu.with_memory_space_constraint(x, pltpu.HBM) for x in operands]
     narrow = pltpu.VMEM((share, ri), BF)
     blocks = pltpu.VMEM((2, BS, BS), BF)
     green_rows = pltpu.VMEM((BS + half, BS), BF)
     result = pl.pallas_call(
         kernel,
         out_shape=jax.ShapeDtypeStruct((2, share, ri), F32),
-        in_specs=[pl.BlockSpec(memory_space=pl.ANY)] * 3 + [pl.BlockSpec(memory_space=pltpu.SMEM)],
+        in_specs=[pl.BlockSpec(memory_space=pl.ANY)] * 4,
         out_specs=pl.BlockSpec(memory_space=pltpu.VMEM),
         scratch_shapes=[
             pltpu.VMEM((2, ri, half, BS), BF),
@@ -329,6 +342,7 @@
             pltpu.VMEM((3, 2 * BS, 2 * BS), BF),
             pltpu.VMEM((256, 256), BF),
             pltpu.VMEM((3 * half, BS), BF),
+            pltpu.SMEM((1, 2), jnp.int32),
             blocks, blocks, green_rows, green_rows,
             pltpu.VMEM((KEEP1, ri, BS), BF),
             pltpu.VMEM((KEEP2, ri, BS), BF),
@@ -338,14 +352,14 @@
             narrow, narrow, narrow, narrow,
             pltpu.VMEM((3, share, ri), F32),
             pltpu.VMEM((3, share, ri), F32),
-            pltpu.SemaphoreType.DMA((4,)),
+            pltpu.SemaphoreType.DMA((5,)),
             pltpu.SemaphoreType.DMA((COPIES,)),
             pltpu.SemaphoreType.DMA((COPIES,)),
         ],
         compiler_params=pltpu.CompilerParams(
             collective_id=0, has_side_effects=True, vmem_limit_bytes=52 * 1024 * 1024
         ),
-    )(tensor, go_blocks, gv_blocks, partners)
+    )(*placed)
     return result[None]
 
 

time: 93.6 us -> 90 us (0.962)
  local copies, waits for them, and re-layouts: 3.04 us -> 0.71 us
  Pallas kernels: 90.3 us -> 89.2 us
    unnamed x7 -> x1, local copies, waits for them, and re-layouts: 3.04 us -> 0.71 us
    pallas_call x1, Pallas kernels: 90.3 us -> 89.2 us  [on_device(): pl.pallas_call(kernel, out_shape=jax.ShapeDtypeStruct((2, share, ri), F32...]
where the time goes in v5:
time: 90 us; the launch traced here: 89.9 us
  Pallas kernels  89.2 us (99%)
    pallas_call x1, Pallas kernels, on_device(): pl.pallas_call(kernel, out_shape=jax.ShapeDtypeStruct((2, share, ri), F32...  89.2 us

profile of v5, /device:TPU:1, one launch (start us, length us, event | category | flops | bytes accessed | tf_op | source)
XLA Modules:
  0.0 89.9 jit_solution(10670325090392366704)
XLA Ops:
  0.0 89.2 %shard_map.46 = f32[2,128,256]{2,1,0:T(8,128)S(1)} custom-call(bf16[1,256,64,128]{3,2,1,0:T(8,128)(2,1)} %tensor.1, bf16[1,2,128,128]{3,2,1,0:T(8,128)(2,1)} %go_hbm.1, bf16[1,2,128,128]{3,2,1,0:T(8,128)(2,1)} %gv_hbm.1, s32[1,2]{1,0:T(1,128)} %partners_hbm.1), custom_call_target="tpu_custom_call" | custom-call | tf_op jit(solution)/shard_map/pallas_call | solution.py:331
  89.2 0.7 copy.6

commit v6 on v5

--- a/solution.py
+++ b/solution.py
@@ -11,10 +11,11 @@
 BS = 128
 
 KEEP1 = 20
-KEEP2 = 22
-RAW_BOUNDS = (0, 8, 16, 24, 32, 38, 42, 44)
+KEEP2 = 23
+RAW_BOUNDS = (0, 8, 16, 24, 32, 38, 41, 44)
+RAW_NEXT = {0: 3, 1: 4, 3: 5, 4: 6}
 FIRST_FROM = 64 - KEEP1
-SECOND_BOUNDS = (42, 52, 60, 64)
+SECOND_BOUNDS = (41, 52, 60, 64)
 P_BOUNDS = (0, 32, 64, 128, 256)
 P_CHUNKS = len(P_BOUNDS) - 1
 
@@ -207,8 +208,8 @@
     second_product([(1, 32)], 0, ri)
     seconds[0].start()
     turn([32, 48])
-    raws[3].start()
-    raws[4].start()
+    raws[0].wait_recv()
+    raws[RAW_NEXT[0]].start()
 
     def wide(ref, at, many):
         return jnp.concatenate([ref[at + j] for j in range(many)], axis=1)
@@ -252,7 +253,10 @@
 
     def raw_chunk(i):
         a, b = RAW_BOUNDS[i], RAW_BOUNDS[i + 1]
-        raws[i].wait_recv()
+        if i > 0:
+            raws[i].wait_recv()
+            if i in RAW_NEXT:
+                raws[RAW_NEXT[i]].start()
         jobs = [(acc_right, trans.at[0], a, far, a)]
         if b <= SECOND_BOUNDS[0]:
             jobs.append((part_left, far, a, trans.at[1], a))
@@ -264,17 +268,15 @@
         contract([(acc_left, rows, a, second, a - SECOND_BOUNDS[0])], b - a, clear=i == 0)
 
     raw_chunk(0)
-    raws[5].start()
+    raw_chunk(1)
     seconds[1].start()
     second_product([(2, 32), (2, 0)], 0, ri)
-    raw_chunk(1)
-    raws[6].start()
+    raw_chunk(2)
     seconds[2].start()
     contract([(acc_self, trans.at[2], 0, rows, 0)], half, clear=True)
     fin_send[SELF] = acc_self[theirs, :]
     finals[SELF].start()
 
-    raw_chunk(2)
     for copy in firsts:
         copy.wait_recv()
     contract([(part_right, first, 0, rows, FIRST_FROM)], KEEP1, clear=True)

time: 90 us -> 90 us (level)
  no operation moved by 1% of the time
where the time goes in v6:
time: 90 us; the launch traced here: 89.9 us
  Pallas kernels  89.2 us (99%)
    pallas_call x1, Pallas kernels, on_device(): pl.pallas_call(kernel, out_shape=jax.ShapeDtypeStruct((2, share, ri), F32...  89.2 us

profile of v6, /device:TPU:1, one launch (start us, length us, event | category | flops | bytes accessed | tf_op | source)
XLA Modules:
  0.0 89.9 jit_solution(11365463799956002573)
XLA Ops:
  0.0 89.2 %shard_map.46 = f32[2,128,256]{2,1,0:T(8,128)S(1)} custom-call(bf16[1,256,64,128]{3,2,1,0:T(8,128)(2,1)} %tensor.1, bf16[1,2,128,128]{3,2,1,0:T(8,128)(2,1)} %go_hbm.1, bf16[1,2,128,128]{3,2,1,0:T(8,128)(2,1)} %gv_hbm.1, s32[1,2]{1,0:T(1,128)} %partners_hbm.1), custom_call_target="tpu_custom_call" | custom-call | tf_op jit(solution)/shard_map/pallas_call | solution.py:333
  89.2 0.7 copy.6

commit v7 on v5

--- a/solution.py
+++ b/solution.py
@@ -15,8 +15,9 @@
 RAW_BOUNDS = (0, 8, 16, 24, 32, 38, 42, 44)
 FIRST_FROM = 64 - KEEP1
 SECOND_BOUNDS = (42, 52, 60, 64)
-P_BOUNDS = (0, 32, 64, 128, 256)
+P_BOUNDS = (0, 16, 32, 64, 128, 256)
 P_CHUNKS = len(P_BOUNDS) - 1
+EARLY_CHUNKS = 2
 
 RIGHT, LEFT, SELF = 0, 1, 2
 
@@ -113,18 +114,6 @@
         copy.wait()
     gsend[pl.ds(0, BS)] = picked(go_ref, left)
     gsend[pl.ds(BS, half)] = nt(choose, picked(gv_ref, left)).astype(BF)
-    green[pl.ds(0, half)] = nt(choose, picked(go_ref, right)).astype(BF)
-    green[pl.ds(2 * half, half)] = nt(choose, picked(go_ref, grid_at)).astype(BF)
-    empty = jnp.zeros((BS, BS), BF)
-
-    def doubled(block):
-        top = jnp.concatenate([block, empty], axis=1)
-        bottom = jnp.concatenate([empty, block], axis=1)
-        return jnp.concatenate([top, bottom], axis=0)
-
-    got2[0] = doubled(picked(gv_ref, right))
-    got2[2] = doubled(picked(gv_ref, grid_at))
-
     def turn(n_blocks):
         width = 64 if len(n_blocks) == 1 else 32
 
@@ -156,25 +145,36 @@
     for copy in siblings[1:]:
         copy.start()
     raws[1].start()
+
+    green[pl.ds(0, half)] = nt(choose, picked(go_ref, right)).astype(BF)
+    green[pl.ds(2 * half, half)] = nt(choose, picked(go_ref, grid_at)).astype(BF)
+    empty = jnp.zeros((BS, BS), BF)
+
+    def doubled(block):
+        top = jnp.concatenate([block, empty], axis=1)
+        bottom = jnp.concatenate([empty, block], axis=1)
+        return jnp.concatenate([top, bottom], axis=0)
+
+    got2[0] = doubled(picked(gv_ref, right))
+    got2[2] = doubled(picked(gv_ref, grid_at))
     loads[1].wait()
 
-    greens.wait_recv()
-    green[pl.ds(half, half)] = gfar[pl.ds(BS, half)]
-    got2[1] = doubled(gfar[pl.ds(0, BS)])
-
-    def first_product(i, carry):
-        p0 = pl.multiple_of(i * 8, 8)
-        tiles = []
-        for j in range(8):
-            tiles.append(traw[0, p0 + j])
-            tiles.append(traw[1, p0 + j])
-        product = nt(green[...], jnp.concatenate(tiles, axis=0)).astype(BF)
-        for j in range(8):
-            occ[p0 + j] = product[:, j * BS:(j + 1) * BS]
-        return carry
+    def first_product(start, stop, row, many):
+        def body(i, carry):
+            p0 = pl.multiple_of(i * 8, 8)
+            tiles = []
+            for j in range(8):
+                tiles.append(traw[0, p0 + j])
+                tiles.append(traw[1, p0 + j])
+            product = nt(green[pl.ds(row, many)], jnp.concatenate(tiles, axis=0)).astype(BF)
+            for j in range(8):
+                occ[p0 + j, pl.ds(row, many)] = product[:, j * BS:(j + 1) * BS]
+            return carry
+
+        lax.fori_loop(start // 8, stop // 8, body, 0)
 
     def second_product(parts, start, size):
-        width = 32 if len(parts) > 1 or size == 32 else 64
+        width = 32 if len(parts) > 1 else min(64, size)
 
         def body(i, carry):
             for direction, n0 in parts:
@@ -199,7 +199,15 @@
     for i in range(P_CHUNKS):
         siblings[i].wait_recv()
         a, b = P_BOUNDS[i], P_BOUNDS[i + 1]
-        lax.fori_loop(a // 8, b // 8, first_product, 0)
+        if i == EARLY_CHUNKS:
+            greens.wait_recv()
+            green[pl.ds(half, half)] = gfar[pl.ds(BS, half)]
+            got2[1] = doubled(gfar[pl.ds(0, BS)])
+            first_product(0, a, half, 2 * half)
+        if i < EARLY_CHUNKS:
+            first_product(a, b, 0, half)
+        else:
+            first_product(a, b, 0, 3 * half)
         second_product([(0, 32)], a, b - a)
         firsts[i].start()
     turn([16])

time: 90 us -> 90 us (level)
  no operation moved by 1% of the time
where the time goes in v7:
time: 90 us; the launch traced here: 89.9 us
  Pallas kernels  89.2 us (99%)
    pallas_call x1, Pallas kernels, on_device(): pl.pallas_call(kernel, out_shape=jax.ShapeDtypeStruct((2, share, ri), F32...  89.2 us

profile of v7, /device:TPU:1, one launch (start us, length us, event | category | flops | bytes accessed | tf_op | source)
XLA Modules:
  0.0 89.9 jit_solution(8973810704562238369)
XLA Ops:
  0.0 89.2 %shard_map.46 = f32[2,128,256]{2,1,0:T(8,128)S(1)} custom-call(bf16[1,256,64,128]{3,2,1,0:T(8,128)(2,1)} %tensor.1, bf16[1,2,128,128]{3,2,1,0:T(8,128)(2,1)} %go_hbm.1, bf16[1,2,128,128]{3,2,1,0:T(8,128)(2,1)} %gv_hbm.1, s32[1,2]{1,0:T(1,128)} %partners_hbm.1), custom_call_target="tpu_custom_call" | custom-call | tf_op jit(solution)/shard_map/pallas_call | solution.py:339
  89.2 0.7 copy.6

commit v8 on v7

--- a/solution.py
+++ b/solution.py
@@ -10,9 +10,9 @@
 F32 = jnp.float32
 BS = 128
 
-KEEP1 = 20
+KEEP1 = 21
 KEEP2 = 22
-RAW_BOUNDS = (0, 8, 16, 24, 32, 38, 42, 44)
+RAW_BOUNDS = (0, 8, 16, 24, 32, 38, 42, 43)
 FIRST_FROM = 64 - KEEP1
 SECOND_BOUNDS = (42, 52, 60, 64)
 P_BOUNDS = (0, 16, 32, 64, 128, 256)
@@ -197,6 +197,9 @@
         lax.fori_loop(start // width, (start + size) // width, body, 0)
 
     for i in range(P_CHUNKS):
+        if i == P_CHUNKS - 1:
+            turn([16])
+            raws[2].start()
         siblings[i].wait_recv()
         a, b = P_BOUNDS[i], P_BOUNDS[i + 1]
         if i == EARLY_CHUNKS:
@@ -210,8 +213,6 @@
             first_product(a, b, 0, 3 * half)
         second_product([(0, 32)], a, b - a)
         firsts[i].start()
-    turn([16])
-    raws[2].start()
     second_product([(1, 32)], 0, ri)
     seconds[0].start()
     turn([32, 48])

time: 90 us -> 90 us (level)
  no operation moved by 1% of the time
where the time goes in v8:
time: 90 us; the launch traced here: 89.9 us
  Pallas kernels  89.2 us (99%)
    pallas_call x1, Pallas kernels, on_device(): pl.pallas_call(kernel, out_shape=jax.ShapeDtypeStruct((2, share, ri), F32...  89.2 us

profile of v8, /device:TPU:1, one launch (start us, length us, event | category | flops | bytes accessed | tf_op | source)
XLA Modules:
  0.0 89.9 jit_solution(5252308785607903621)
XLA Ops:
  0.0 89.2 %shard_map.46 = f32[2,128,256]{2,1,0:T(8,128)S(1)} custom-call(bf16[1,256,64,128]{3,2,1,0:T(8,128)(2,1)} %tensor.1, bf16[1,2,128,128]{3,2,1,0:T(8,128)(2,1)} %go_hbm.1, bf16[1,2,128,128]{3,2,1,0:T(8,128)(2,1)} %gv_hbm.1, s32[1,2]{1,0:T(1,128)} %partners_hbm.1), custom_call_target="tpu_custom_call" | custom-call | tf_op jit(solution)/shard_map/pallas_call | solution.py:340
  89.2 0.7 copy.6

commit v9 on v8

--- a/solution.py
+++ b/solution.py
@@ -115,7 +115,7 @@
     gsend[pl.ds(0, BS)] = picked(go_ref, left)
     gsend[pl.ds(BS, half)] = nt(choose, picked(gv_ref, left)).astype(BF)
     def turn(n_blocks):
-        width = 64 if len(n_blocks) == 1 else 32
+        width = 128 if len(n_blocks) == 1 else 64
 
         def body(i, carry):
             for n0 in n_blocks:
@@ -161,20 +161,20 @@
 
     def first_product(start, stop, row, many):
         def body(i, carry):
-            p0 = pl.multiple_of(i * 8, 8)
+            p0 = pl.multiple_of(i * 16, 16)
             tiles = []
-            for j in range(8):
+            for j in range(16):
                 tiles.append(traw[0, p0 + j])
                 tiles.append(traw[1, p0 + j])
             product = nt(green[pl.ds(row, many)], jnp.concatenate(tiles, axis=0)).astype(BF)
-            for j in range(8):
+            for j in range(16):
                 occ[p0 + j, pl.ds(row, many)] = product[:, j * BS:(j + 1) * BS]
             return carry
 
-        lax.fori_loop(start // 8, stop // 8, body, 0)
+        lax.fori_loop(start // 16, stop // 16, body, 0)
 
     def second_product(parts, start, size):
-        width = 32 if len(parts) > 1 else min(64, size)
+        width = 64 if len(parts) > 1 else min(128, size)
 
         def body(i, carry):
             for direction, n0 in parts:

time: 90 us -> 90 us (level)
  no operation moved by 1% of the time
where the time goes in v9:
time: 90 us; the launch traced here: 89.9 us
  Pallas kernels  89.2 us (99%)
    pallas_call x1, Pallas kernels, on_device(): pl.pallas_call(kernel, out_shape=jax.ShapeDtypeStruct((2, share, ri), F32...  89.2 us

profile of v9, /device:TPU:1, one launch (start us, length us, event | category | flops | bytes accessed | tf_op | source)
XLA Modules:
  0.0 89.9 jit_solution(17525710450645888166)
XLA Ops:
  0.0 89.2 %shard_map.46 = f32[2,128,256]{2,1,0:T(8,128)S(1)} custom-call(bf16[1,256,64,128]{3,2,1,0:T(8,128)(2,1)} %tensor.1, bf16[1,2,128,128]{3,2,1,0:T(8,128)(2,1)} %go_hbm.1, bf16[1,2,128,128]{3,2,1,0:T(8,128)(2,1)} %gv_hbm.1, s32[1,2]{1,0:T(1,128)} %partners_hbm.1), custom_call_target="tpu_custom_call" | custom-call | tf_op jit(solution)/shard_map/pallas_call | solution.py:340
  89.2 0.7 copy.6

commit v10 on v9

--- a/solution.py
+++ b/solution.py
@@ -12,9 +12,9 @@
 
 KEEP1 = 21
 KEEP2 = 22
-RAW_BOUNDS = (0, 8, 16, 24, 32, 38, 42, 43)
+RAW_BOUNDS = (0, 8, 16, 24, 32, 40, 42, 43)
 FIRST_FROM = 64 - KEEP1
-SECOND_BOUNDS = (42, 52, 60, 64)
+SECOND_BOUNDS = (42, 54, 62, 64)
 P_BOUNDS = (0, 16, 32, 64, 128, 256)
 P_CHUNKS = len(P_BOUNDS) - 1
 EARLY_CHUNKS = 2

time: 90 us -> 90 us (level)
  no operation moved by 1% of the time
where the time goes in v10:
time: 90 us; the launch traced here: 89.8 us
  Pallas kernels  89.1 us (99%)
    pallas_call x1, Pallas kernels, on_device(): pl.pallas_call(kernel, out_shape=jax.ShapeDtypeStruct((2, share, ri), F32...  89.1 us

profile of v10, /device:TPU:1, one launch (start us, length us, event | category | flops | bytes accessed | tf_op | source)
XLA Modules:
  0.0 89.8 jit_solution(8567570880645446347)
XLA Ops:
  0.0 89.1 %shard_map.46 = f32[2,128,256]{2,1,0:T(8,128)S(1)} custom-call(bf16[1,256,64,128]{3,2,1,0:T(8,128)(2,1)} %tensor.1, bf16[1,2,128,128]{3,2,1,0:T(8,128)(2,1)} %go_hbm.1, bf16[1,2,128,128]{3,2,1,0:T(8,128)(2,1)} %gv_hbm.1, s32[1,2]{1,0:T(1,128)} %partners_hbm.1), custom_call_target="tpu_custom_call" | custom-call | tf_op jit(solution)/shard_map/pallas_call | solution.py:340
  89.1 0.7 copy.6
